TPU v7x, 32 devices: a whole 2x2x4 slice. The times are simulated.
32 devices in a mesh: fsdp: 2 (over core), expert: 16 (over z, y, x).
Axes of the slice: x: 2, y: 2, z: 4, core: 2. Of those that a mesh axis runs over, the one named last changes fastest.
Arguments:
- tokens: bfloat16 [3, 256, 7168], P(None, 'expert'), may hold values from -6 to 6
- route_ids: int32 [3, 256, 8], P(None, 'expert'), may hold values from 0 to 15, all different within a row; in each aligned block of 16 rows (0 to 15, 16 to 31, ..., all dimensions but the last counted through in order) at most 12 rows name the same one
- gate_values: bfloat16 [3, 256, 8], P(None, 'expert'), may hold values from 0.25 to 1
- cap_limit: int32 [16], replicated, may hold values from 6 to 12
- update_ids: int32 [16], replicated, may hold values from 0 to 15, each once
- expert_weights: bfloat16 [16, 7168, 3072], P(None, ('fsdp', 'expert')), may hold values from -0.109375 to 0.109375
Outputs:
- moe_output: bfloat16 [3, 256, 7168], P(None, 'expert', 'fsdp')
Inputs may be any that keep to these rules, and one draw needn't show every extreme that they name: `route_ids`: each row names 8 different experts. In every aligned block of 16 rows of one step (the rows of one device) no expert is named by more than 12 rows, a bound that some block reaches. `update_ids`: each expert once.
All inputs are finite; a program needn't handle non-finite values.
Results may differ from a plain program's by a relative error of at most 0.0058.
Values may be sent and summed in bfloat16 or wider, within the bound.
A program may use at most 192 MiB of HBM per device.

v0:
```python
import jax
import jax.numpy as jnp
from jax import lax
from jax.sharding import PartitionSpec as P


def slot_tables(route_block, gate_block, cap_limit, slot_count):
    row_count, top_count = route_block.shape
    experts = cap_limit.shape[0]
    flat_ids = route_block.reshape(row_count * top_count)
    expert_hot = (flat_ids[:, None] == jnp.arange(experts, dtype=jnp.int32)[None, :]).astype(
        jnp.int32
    )
    running = jnp.cumsum(expert_hot, axis=0) - 1
    position = jnp.sum(running * expert_hot, axis=1)
    limit_row = jnp.sum(expert_hot * cap_limit[None, :], axis=1)
    kept_mask = position < limit_row
    slot_index = flat_ids * slot_count + position
    slot_match = slot_index[:, None] == jnp.arange(experts * slot_count, dtype=jnp.int32)[None, :]
    slot_hot = jnp.where(kept_mask[:, None], slot_match, False).astype(jnp.bfloat16)
    row_match = (
        jnp.arange(row_count * top_count, dtype=jnp.int32)[:, None] // top_count
        == jnp.arange(row_count, dtype=jnp.int32)[None, :]
    )
    row_hot = row_match.astype(jnp.bfloat16)
    dispatch_mat = lax.dot_general(
        slot_hot, row_hot, (((0,), (0,)), ((), ())), preferred_element_type=jnp.float32
    ).astype(jnp.bfloat16)
    weighted = slot_hot * gate_block.reshape(row_count * top_count)[:, None]
    combine_mat = lax.dot_general(
        row_hot, weighted, (((0,), (0,)), ((), ())), preferred_element_type=jnp.float32
    ).astype(jnp.bfloat16)
    return (dispatch_mat, combine_mat)


def body(tokens, route_ids, gate_values, cap_limit, update_ids, expert_weights):
    step_count, row_count, model_width = tokens.shape
    top_count = route_ids.shape[2]
    experts = cap_limit.shape[0]
    fsdp_count = lax.axis_size("fsdp")
    slot_count = min(row_count, 3 * row_count * top_count // (2 * experts))
    local_rows = expert_weights.shape[1]
    hidden_all = expert_weights.shape[2] // 3
    hidden_share = hidden_all // fsdp_count
    inverse_order = jnp.argsort(update_ids)
    ordered = jnp.take(expert_weights, inverse_order, axis=0)
    pieces = ordered.reshape(experts, local_rows, 3, fsdp_count, hidden_share)
    pieces = jnp.transpose(pieces, (3, 0, 1, 2, 4))
    outgoing = pieces.reshape(fsdp_count * experts, local_rows, 3 * hidden_share)
    arrived = lax.all_to_all(outgoing, ("fsdp", "expert"), split_axis=0, concat_axis=0, tiled=True)
    owned_block = arrived.reshape(model_width, 3, hidden_share)
    gate_w = owned_block[:, 0, :]
    up_w = owned_block[:, 1, :]
    down_t = owned_block[:, 2, :]
    results = []
    for step_index in range(step_count):
        dispatch_mat, combine_mat = slot_tables(
            route_ids[step_index], gate_values[step_index], cap_limit, slot_count
        )
        sending = jnp.dot(
            dispatch_mat, tokens[step_index], preferred_element_type=jnp.float32
        ).astype(jnp.bfloat16)
        sending = sending.reshape(experts, slot_count, model_width)
        received = lax.all_to_all(sending, "expert", split_axis=0, concat_axis=0, tiled=True)
        item_count = received.shape[1]
        flat_rows = received.reshape(-1, model_width)
        gate_part = jnp.dot(flat_rows, gate_w, preferred_element_type=jnp.float32)
        up_part = jnp.dot(flat_rows, up_w, preferred_element_type=jnp.float32)
        hidden = (jax.nn.silu(gate_part) * up_part).astype(jnp.bfloat16)
        partial_out = lax.dot_general(
            hidden, down_t, (((1,), (1,)), ((), ())), preferred_element_type=jnp.float32
        )
        partial_out = partial_out.reshape(received.shape[0], item_count, model_width)
        reduced = lax.psum_scatter(partial_out, "fsdp", scatter_dimension=2, tiled=True).astype(
            jnp.bfloat16
        )
        returned = lax.all_to_all(reduced, "expert", split_axis=0, concat_axis=0, tiled=True)
        mixed_rows = jnp.dot(
            combine_mat,
            returned.reshape(experts * slot_count, -1),
            preferred_element_type=jnp.float32,
        )
        results.append(mixed_rows.astype(jnp.bfloat16))
    return jnp.stack(results)


def solution(mesh):
    return jax.shard_map(
        body,
        mesh=mesh,
        in_specs=(
            P(None, "expert", None),
            P(None, "expert", None),
            P(None, "expert", None),
            P(),
            P(),
            P(None, ("fsdp", "expert"), None),
        ),
        out_specs=P(None, "expert", "fsdp"),
        check_vma=False,
    )
```

profile of v0, /device:TPU:0, one launch (start us, length us, event | category | flops | bytes accessed | tf_op | source)
XLA Modules:
  0.0 1272.3 jit_solution(4340692127670341773)
XLA Ops:
  6.5 0.7 fusion.145
  7.4 0.1 fusion.77
  7.7 0.1 fusion.72
  7.8 0.2 reduce_window_sum.20
  8.0 0.2 reduce_window_sum.24
  8.4 0.2 reduce_window_sum.25
  8.6 1.5 select_reduce_fusion.4
  10.1 2.1 convolution_convert_fusion.2
  12.2 2.6 reshape.129
  14.8 8.4 all-to-all-start
  23.2 1.3 sort.17
  24.5 16.3 %gather_fusion = bf16[16,224,3072]{2,1,0:T(8,128)(2,1)} fusion(bf16[16,224,3072]{2,1,0:T(8,128)(2,1)} %param.11, s32[1024]{0:T(1024)S(1)} %pad_clamp_fusion), kind=kCustom, calls=%fused_computation | custom fusion | bytes 44040256 | tf_op jit(solution)/shard_map/jit(_take)/gather | solution.py:46
  40.8 48.4 %gather.7 = bf16[16,224,3,2,512]{4,3,2,1,0:T(2,128)(2,1)} reshape(bf16[16,224,3072]{2,1,0:T(8,128)(2,1)} %gather_fusion) | data formatting | bytes 44040192 | tf_op jit(solution)/shard_map/jit(_take)/gather | solution.py:46
  89.2 60.1 %copy.33 = bf16[16,224,3,2,512]{1,4,2,0,3:T(8,128)(2,1)} copy(bf16[16,224,3,2,512]{4,3,2,1,0:T(2,128)(2,1)} %gather.7) | data formatting | bytes 44040192 | tf_op jit(solution)/shard_map/jit(_take)/gather | solution.py:46
  149.3 21.3 %broadcast_select_fusion = bf16[16,224,3,2,512]{1,4,2,0,3:T(8,128)(2,1)} fusion(bf16[16,224,3,2,512]{1,4,2,0,3:T(8,128)(2,1)} %copy.33, pred[16]{0:T(512)(128)(4,1)S(1)} %compare_and_fusion), kind=kLoop, calls=%fused_computation.1 | loop fusion | flops 11010048 | bytes 44040208 | tf_op jit(solution)/shard_map/jit(_take)/select_n | solution.py:46
  170.6 28.8 %copy.34 = bf16[32,224,1536]{2,1,0:T(8,128)(2,1)} copy(bf16[32,224,1536]{1,2,0:T(8,128)(2,1)} %bitcast.59) | data formatting | bytes 44040192 | tf_op jit(solution)/shard_map/reshape | solution.py:49
  199.4 6.0 all-to-all-start.1
  205.4 0.2 reduce-scatter.4.cloned.1.call-start
  205.6 3.0 reshape.130
  208.6 484.8 %all-to-all-done.1 = bf16[32,224,1536]{2,1,0:T(8,128)(2,1)} async-done(((bf16[32,224,1536]{2,1,0:T(8,128)(2,1)}), bf16[32,224,1536]{2,1,0:T(8,128)(2,1)}, u32[]{:S(2)}, u32[]{:S(2)}) %all-to-all-start.1) | async-done | bytes 22020128 | tf_op jit(solution)/shard_map/all_to_all | solution.py:50
  693.5 62.3 %reshape.150 = bf16[7168,3,512]{2,1,0:T(4,128)(2,1)} reshape(bf16[32,224,1536]{2,1,0:T(8,128)(2,1)} %all-to-all-done.1) | data formatting | bytes 44040192 | tf_op jit(solution)/shard_map/reshape | solution.py:51
  755.8 48.1 %fusion.144 = (bf16[7168,1,512]{2,1,0:T(2,128)(2,1)}, bf16[7168,1,512]{2,1,0:T(2,128)(2,1)}, bf16[7168,1,512]{2,1,0:T(2,128)(2,1)}) fusion(bf16[7168,3,512]{2,1,0:T(4,128)(2,1)} %reshape.150), kind=kLoop, calls=%fused_computation.120 | loop fusion | bytes 44040192 | tf_op jit(solution)/shard_map/slice | solution.py:54
  804.0 30.7 %copy.49 = bf16[7168,1,512]{0,2,1:T(8,128)(2,1)} copy(bf16[7168,1,512]{2,1,0:T(2,128)(2,1)} %get-tuple-element.14) | data formatting | bytes 14680064
  834.7 30.8 %copy.50 = bf16[7168,1,512]{0,2,1:T(8,128)(2,1)} copy(bf16[7168,1,512]{2,1,0:T(2,128)(2,1)} %get-tuple-element.15) | data formatting | bytes 14680064
  865.4 5.8 fusion.10
  871.2 2.6 fusion.30
  873.8 10.2 fusion.43
  884.1 2.1 convolution_convert_fusion.1
  886.2 2.6 reshape.134
  888.8 94.9 %all_to_all.35 = bf16[16,12,7168]{2,1,0:T(8,128)(2,1)} all-to-all(bf16[16,12,7168]{2,1,0:T(8,128)(2,1)} %reshape.134), channel_id=1, replica_groups=mesh['fsdp'=2,'expert'=16] {'expert'}, dimensions={0} | all-to-all | bytes 5505024 | tf_op jit(solution)/shard_map/all_to_all | solution.py:64
  983.7 4.6 reshape.135
  988.4 6.6 fusion.8
  995.0 2.7 fusion.27
  997.8 10.2 fusion.41
  1008.1 0.6 copy-done.10
  1008.7 2.1 convolution_convert_fusion
  1010.8 2.6 reshape.137
  1013.4 85.9 %all_to_all.36 = bf16[16,12,7168]{2,1,0:T(8,128)(2,1)} all-to-all(bf16[16,12,7168]{2,1,0:T(8,128)(2,1)} %reshape.137), channel_id=1, replica_groups=mesh['fsdp'=2,'expert'=16] {'expert'}, dimensions={0} | all-to-all | bytes 5505024 | tf_op jit(solution)/shard_map/all_to_all | solution.py:64
  1099.3 4.6 reshape.138
  1103.9 6.6 fusion.6
  1110.6 2.7 fusion.24
  1113.4 10.2 fusion.39
  1123.6 1.9 convert_element_type.74
  1125.5 2.1 copy.38
  1127.6 3.9 all-to-all-start.2
  1131.6 2.4 convert_element_type.81
  1134.0 2.0 copy.42
  1136.0 33.0 %all-to-all-done.2 = bf16[16,12,3584]{2,1,0:T(8,128)(2,1)S(1)} async-done(((bf16[16,12,3584]{2,1,0:T(8,128)(2,1)}), bf16[16,12,3584]{2,1,0:T(8,128)(2,1)S(1)}, u32[]{:S(2)}, u32[]{:S(2)}) %all-to-all-start.2) | async-done | bytes 1376288 | tf_op jit(solution)/shard_map/all_to_all | solution.py:77
  1169.0 8.6 all-to-all-start.4
  1177.6 1.9 convert_element_type.88
  1179.5 2.1 copy.46
  1181.6 34.1 %all-to-all-done.4 = bf16[16,12,3584]{2,1,0:T(8,128)(2,1)} async-done(((bf16[16,12,3584]{2,1,0:T(8,128)(2,1)}), bf16[16,12,3584]{2,1,0:T(8,128)(2,1)}, u32[]{:S(2)}, u32[]{:S(2)}) %all-to-all-start.4) | async-done | bytes 1376288 | tf_op jit(solution)/shard_map/all_to_all | solution.py:77
  1215.6 8.5 all-to-all-start.6
  1224.2 0.1 mul.103
  1224.4 0.1 mul.111
  1224.6 0.1 mul.119
  1224.7 0.4 reshape.133
  1225.1 2.4 reshape.136
  1227.5 0.5 fusion.12
  1228.0 0.5 fusion.13
  1228.5 33.5 %all-to-all-done.6 = bf16[16,12,3584]{2,1,0:T(8,128)(2,1)} async-done(((bf16[16,12,3584]{2,1,0:T(8,128)(2,1)}), bf16[16,12,3584]{2,1,0:T(8,128)(2,1)}, u32[]{:S(2)}, u32[]{:S(2)}) %all-to-all-start.6) | async-done | bytes 1376288 | tf_op jit(solution)/shard_map/all_to_all | solution.py:77
  1262.1 2.4 reshape.139
  1264.4 0.5 fusion.14
  1265.0 0.8 pad_maximum_fusion
  (69 shorter events, 1.3 us)
Async XLA Ops:
  8.3 1.8 copy-start.4
  10.1 4.7 copy-start.6
  10.1 4.7 copy-start.8
  12.2 11.0 copy-start.12
  14.8 184.6 %all-to-all-start = ((bf16[16,12,7168]{2,1,0:T(8,128)(2,1)}), bf16[16,12,7168]{2,1,0:T(8,128)(2,1)}, u32[]{:S(2)}, u32[]{:S(2)}) async-start(bf16[16,12,7168]{2,1,0:T(8,128)(2,1)} %reshape.129), calls=%async_computation | async-start | bytes 7340032 | tf_op jit(solution)/shard_map/all_to_all | solution.py:64
  199.4 494.1 %all-to-all-start.1 = ((bf16[32,224,1536]{2,1,0:T(8,128)(2,1)}), bf16[32,224,1536]{2,1,0:T(8,128)(2,1)}, u32[]{:S(2)}, u32[]{:S(2)}) async-start(bf16[32,224,1536]{2,1,0:T(8,128)(2,1)} %copy.34), calls=%async_computation.1 | async-start | bytes 44040192 | tf_op jit(solution)/shard_map/all_to_all | solution.py:50
  205.4 918.2 %reduce-scatter.4.cloned.1.call-start = ((), (), s32[]{:S(2)}) async-start(), calls=%async_computation.10 | async-start | bytes 8257536 | tf_op jit(solution)/shard_map/reduce_scatter | solution.py:74
  865.4 5.8 copy-start
  884.0 247.5 %reduce-scatter.6.cloned.1.call-start = ((), (), s32[]{:S(2)}) async-start(), calls=%async_computation.11 | async-start | bytes 8257536 | tf_op jit(solution)/shard_map/reduce_scatter | solution.py:74
  983.7 11.3 slice-start
  988.4 6.6 slice-start.1
  988.4 6.7 copy-start.2
  1008.0 0.7 copy-start.10
  1008.0 0.7 copy-start.11
  1008.0 0.7 copy-start.5
  1008.1 169.5 %reduce-scatter.8.cloned.1.call-start = ((), (), s32[]{:S(2)}) async-start(), calls=%async_computation.12 | async-start | bytes 8257536 | tf_op jit(solution)/shard_map/reduce_scatter | solution.py:74
  1099.3 11.3 slice-start.2
  1103.9 6.6 slice-start.3
  1103.9 6.6 copy-start.1
  1127.6 41.3 %all-to-all-start.2 = ((bf16[16,12,3584]{2,1,0:T(8,128)(2,1)}), bf16[16,12,3584]{2,1,0:T(8,128)(2,1)S(1)}, u32[]{:S(2)}, u32[]{:S(2)}) async-start(bf16[16,12,3584]{2,1,0:T(8,128)(2,1)} %copy.38), calls=%async_computation.3 | async-start | bytes 3670016 | tf_op jit(solution)/shard_map/all_to_all | solution.py:77
  1169.0 46.7 %all-to-all-start.4 = ((bf16[16,12,3584]{2,1,0:T(8,128)(2,1)}), bf16[16,12,3584]{2,1,0:T(8,128)(2,1)}, u32[]{:S(2)}, u32[]{:S(2)}) async-start(bf16[16,12,3584]{2,1,0:T(8,128)(2,1)} %copy.42), calls=%async_computation.6 | async-start | bytes 3670016 | tf_op jit(solution)/shard_map/all_to_all | solution.py:77
  1177.5 46.6 %copy-start.3 = (bf16[3,16,8]{1,2,0:T(8,128)(2,1)S(1)}, bf16[3,16,8]{1,2,0:T(8,128)(2,1)}, u32[]{:S(2)}) copy-start(bf16[3,16,8]{1,2,0:T(8,128)(2,1)} %param.8) | copy-start | bytes 2308
  1181.6 45.9 %copy-start.7 = (s32[128]{0:T(128)S(1)}, s32[128]{0:T(128)}, u32[]{:S(2)}) copy-start(s32[128]{0:T(128)} %copy-done.6) | copy-start | bytes 1540
  1181.6 45.9 %copy-start.9 = (pred[128]{0:T(512)(128)(4,1)S(1)}, pred[128]{0:T(512)(128)(4,1)}, u32[]{:S(2)}) copy-start(pred[128]{0:T(512)(128)(4,1)} %copy-done.8) | copy-start | bytes 388
  1215.6 46.4 %all-to-all-start.6 = ((bf16[16,12,3584]{2,1,0:T(8,128)(2,1)}), bf16[16,12,3584]{2,1,0:T(8,128)(2,1)}, u32[]{:S(2)}, u32[]{:S(2)}) async-start(bf16[16,12,3584]{2,1,0:T(8,128)(2,1)} %copy.46), calls=%async_computation.9 | async-start | bytes 3670016 | tf_op jit(solution)/shard_map/all_to_all | solution.py:77
Sparse Core Ops, SparseCore 0:
  884.1 19.9 reduce-scatter.3
  1008.2 11.8 reduce-scatter.5
  1123.7 11.7 reduce-scatter.7
where the time goes:
time: 1280 us; the launch traced here: 1270 us
  waiting for transfers between devices  586 us (46%)
  local copies, waits for them, and re-layouts  359 us (28%)
  blocking collectives  181 us (14%)
  matrix products  65.5 us (5%)
  starting transfers between devices  35.6 us (3%)
  other arithmetic  32 us (2%)
  between operations  13.5 us (1%)
    all_to_all x1, waiting for transfers between devices, body(): lax.all_to_all(outgoing, ('fsdp', 'expert'), split_axis=0, concat_axis=0,...  485 us
    all_to_all x2, blocking collectives, body(): lax.all_to_all(sending, 'expert', split_axis=0, concat_axis=0, tiled=True)  181 us
    gather x3, local copies, waits for them, and re-layouts, body(): ordered = jnp.take(expert_weights, inverse_order, axis=0)  125 us
    all_to_all x3, waiting for transfers between devices, body(): lax.all_to_all(reduced, 'expert', split_axis=0, concat_axis=0, tiled=True)  101 us
    reshape x1, local copies, waits for them, and re-layouts, body(): owned_block = arrived.reshape(model_width, 3, hidden_share)  62.3 us
    unnamed x36, local copies, waits for them, and re-layouts  62.1 us
    slice x1, local copies, waits for them, and re-layouts, body(): down_t = owned_block[:, 2, :]  48.1 us
    dot_general x3, matrix products, body(): lax.dot_general(hidden, down_t, (((1,), (1,)), ((), ())), preferred_eleme...  30.5 us
  transfers between devices with their start and end apart: 8, of which 4 were waited for; matrix products, arithmetic and copies ran while one was open for 20% of the time, Pallas kernels for 0%

commit v1 on v0

v1 whole, which is shorter than its diff:
```python
import functools

import jax
import jax.numpy as jnp
from jax import lax
from jax.experimental import pallas as pl
from jax.experimental.pallas import tpu as pltpu
from jax.sharding import PartitionSpec as P

TILE = 128
ALIGN = 16
BF16 = jnp.bfloat16
F32 = jnp.float32


def dot(a, b, ca=1, cb=0):
    return lax.dot_general(a, b, (((ca,), (cb,)), ((), ())), preferred_element_type=F32)


def tables(route_ids, gate_values, cap_limit, block_rows):
    rows = route_ids.shape[0]
    experts = cap_limit.shape[0]
    hot = route_ids[:, :, None] == jnp.arange(experts, dtype=jnp.int32)[None, None, :]
    chosen = jnp.any(hot, axis=1)
    gates = jnp.sum(jnp.where(hot, gate_values[:, :, None].astype(F32), 0.0), axis=1)
    at = jnp.arange(rows, dtype=jnp.int32)
    earlier = at[None, :] < at[:, None]
    same = at[None, :] // block_rows == at[:, None] // block_rows
    position = dot((earlier & same).astype(BF16), chosen.astype(BF16)).astype(jnp.int32)
    kept = chosen & (position < cap_limit[None, :])
    before = dot(earlier.astype(BF16), kept.astype(BF16)).astype(jnp.int32)
    counts = jnp.sum(kept.astype(jnp.int32), axis=0)
    padded = (counts + (ALIGN - 1)) // ALIGN * ALIGN
    es = jnp.arange(experts, dtype=jnp.int32)
    starts = jnp.sum(jnp.where(es[None, :] < es[:, None], padded[None, :], 0), axis=1)
    slots = jnp.where(kept, before + starts[None, :], -1)
    chunks = (counts + (TILE - 1)) // TILE
    return slots.T[:, None, :], gates.T[:, None, :], starts, chunks


def up_kernel(parts, starts, chunks, order, mine, slots_ref, x_ref, *refs):
    weights, out_ref = refs[:-1], refs[-1]
    e = pl.program_id(0)
    local = x_ref.shape[2]

    @pl.when(e == 0)
    def _():
        out_ref[...] = jnp.zeros_like(out_ref)

    slots = slots_ref[0]

    def step(c, carry):
        base = pl.multiple_of(starts[e] + c * TILE, ALIGN)
        pick = slots == base + lax.broadcasted_iota(jnp.int32, (TILE, slots.shape[1]), 0)
        pick = pick.astype(F32).astype(BF16)
        a = b = None
        for i in range(parts):
            xs = dot(pick, x_ref[i]).astype(BF16)
            da = dot(xs, weights[2 * i][0])
            db = dot(xs, weights[2 * i + 1][0])
            a, b = (da, db) if a is None else (a + da, b + db)
        out_ref[0, pl.ds(base, TILE), :] = a.astype(out_ref.dtype)
        out_ref[1, pl.ds(base, TILE), :] = b.astype(out_ref.dtype)
        return carry

    lax.fori_loop(0, chunks[e], step, 0)


def down_kernel(parts, starts, chunks, order, mine, slots_ref, gates_ref, h_ref, *refs):
    weights, out_ref = refs[:-1], refs[-1]
    e = pl.program_id(0)
    total = h_ref.shape[0]

    @pl.when(e == 0)
    def _():
        out_ref[...] = jnp.zeros_like(out_ref)

    slots = slots_ref[0]
    gates = gates_ref[0]

    def step(c, carry):
        first = starts[e] + c * TILE
        base = pl.multiple_of(jnp.minimum(first, total - TILE), ALIGN)
        number = base + lax.broadcasted_iota(jnp.int32, (TILE, slots.shape[1]), 0)
        mix = jnp.where((slots == number) & (number >= first), gates, 0.0).astype(BF16)
        h = h_ref[pl.ds(base, TILE), :]
        for i in range(parts):
            y = dot(h, weights[i][0], 1, 1)
            high = y.astype(BF16)
            low = (y - high.astype(F32)).astype(BF16)
            out_ref[i] += dot(mix, high, 0, 0) + dot(mix, low, 0, 0)
        return carry

    lax.fori_loop(0, chunks[e], step, 0)


def halving(part, order):
    n = part.shape[0]
    bits = n.bit_length() - 1
    me = lax.axis_index("expert")
    cur = part.reshape((2,) * bits + part.shape[1:])
    left = list(range(bits - 1, -1, -1))
    for b in order:
        axis = left.index(b)
        bit = (me >> b) & 1
        send = lax.dynamic_index_in_dim(cur, 1 - bit, axis, keepdims=False).astype(BF16)
        keep = lax.dynamic_index_in_dim(cur, bit, axis, keepdims=False).astype(F32)
        got = lax.ppermute(send, "expert", [(i, i ^ (1 << b)) for i in range(n)])
        cur = keep + got.astype(F32)
        left.pop(axis)
    return cur


def body(tokens, route_ids, gate_values, cap_limit, update_ids, expert_weights):
    steps, block_rows, width = tokens.shape
    top = route_ids.shape[2]
    experts = cap_limit.shape[0]
    parts = lax.axis_size("fsdp")
    owners = lax.axis_size("expert")
    local = expert_weights.shape[1]
    hidden = expert_weights.shape[2] // 3
    share = hidden // parts
    rows = steps * owners * block_rows
    f = lax.axis_index("fsdp")

    es = jnp.arange(experts, dtype=jnp.int32)
    order = jnp.sum(jnp.where(update_ids[None, :] == es[:, None], es[None, :], 0), axis=1)
    ids = lax.all_gather(route_ids, "expert", axis=1, tiled=True).reshape(rows, top)
    gate = lax.all_gather(gate_values, "expert", axis=1, tiled=True).reshape(rows, top)
    slots, gates, starts, chunks = tables(ids, gate, cap_limit, block_rows)

    x = tokens.reshape(steps, block_rows, parts, owners, local)
    x = jnp.transpose(x, (3, 2, 0, 1, 4))
    x = lax.all_to_all(x, "expert", split_axis=0, concat_axis=0, tiled=True)
    x = jnp.transpose(x, (1, 2, 0, 3, 4)).reshape(parts, rows, local)

    others = []
    for s in range(1, parts):
        to = (f + s) % parts
        cut = expert_weights.reshape(experts, local, 3, parts, share)
        cut = lax.dynamic_index_in_dim(cut, to, 3, keepdims=False)
        cut = jnp.transpose(cut, (2, 0, 1, 3))
        others.append(lax.ppermute(cut, "fsdp", [(i, (i + s) % parts) for i in range(parts)]))
    sources = [(f - s) % parts for s in range(parts)]
    x = jnp.stack([lax.dynamic_index_in_dim(x, i, 0, keepdims=False) for i in sources])

    packed = -(-(rows * top + experts * (ALIGN - 1)) // (ALIGN * owners)) * ALIGN * owners
    mine = f.astype(jnp.int32).reshape(1)
    whole = lambda *shape: pl.BlockSpec(shape, lambda e, *_: (0,) * len(shape))
    line = pl.BlockSpec((1, 1, rows), lambda e, *_: (e, 0, 0))

    def own(kind):
        return pl.BlockSpec((1, local, share), lambda e, st, ch, od, mi: (od[e], 0, kind * parts + mi[0]))

    def other(kind):
        return pl.BlockSpec((None, 1, local, share), lambda e, st, ch, od, mi: (kind, od[e], 0, 0))

    scalars = (starts, chunks, order, mine)
    params = pltpu.CompilerParams(vmem_limit_bytes=58 * 2**20)
    up_specs, up_args, down_specs, down_args = [own(0), own(1)], [expert_weights] * 2, [own(2)], [expert_weights]
    for got in others:
        up_specs += [other(0), other(1)]
        up_args += [got, got]
        down_specs.append(other(2))
        down_args.append(got)

    ab = pl.pallas_call(
        functools.partial(up_kernel, parts),
        out_shape=jax.ShapeDtypeStruct((2, packed + TILE, share), BF16),
        grid_spec=pltpu.PrefetchScalarGridSpec(
            num_scalar_prefetch=4,
            grid=(experts,),
            in_specs=[line, whole(parts, rows, local)] + up_specs,
            out_specs=whole(2, packed + TILE, share),
        ),
        compiler_params=params,
        cost_estimate=pl.CostEstimate(flops=2 * packed * local * parts * 2 * share, bytes_accessed=3 * 10**7, transcendentals=0),
    )(*scalars, slots, x, *up_args)

    bits = owners.bit_length() - 1
    down_order = list(range(2, bits))[::-1]
    a = halving(ab[0, :packed].reshape(owners, packed // owners, share), [0, 1] + down_order)
    b = halving(ab[1, :packed].reshape(owners, packed // owners, share), [1, 0] + down_order)
    h = (a * jax.nn.sigmoid(a) * b).astype(BF16)
    h = lax.all_gather(h, "expert", axis=0, tiled=True)

    out = pl.pallas_call(
        functools.partial(down_kernel, parts),
        out_shape=jax.ShapeDtypeStruct((parts, rows, local), F32),
        grid_spec=pltpu.PrefetchScalarGridSpec(
            num_scalar_prefetch=4,
            grid=(experts,),
            in_specs=[line, line, whole(packed, share)] + down_specs,
            out_specs=whole(parts, rows, local),
        ),
        compiler_params=params,
        cost_estimate=pl.CostEstimate(flops=2 * packed * local * parts * (share + 2 * rows), bytes_accessed=2 * 10**7, transcendentals=0),
    )(*scalars, slots, gates, h, *down_args)

    total = lax.dynamic_index_in_dim(out, 0, 0, keepdims=False)
    for s in range(1, parts):
        total = total + lax.ppermute(out[s], "fsdp", [(i, (i - s) % parts) for i in range(parts)])
    y = total.astype(BF16).reshape(steps, owners, block_rows, local)
    y = lax.all_to_all(y, "expert", split_axis=1, concat_axis=1, tiled=True)
    return jnp.transpose(y, (0, 2, 1, 3)).reshape(steps, block_rows, owners * local)


def solution(mesh):
    return jax.shard_map(
        body,
        mesh=mesh,
        in_specs=(
            P(None, "expert", None),
            P(None, "expert", None),
            P(None, "expert", None),
            P(),
            P(),
            P(None, ("fsdp", "expert"), None),
        ),
        out_specs=P(None, "expert", "fsdp"),
        check_vma=False,
    )
```

time: 1280 us -> 576 us (0.45)
  waiting for transfers between devices: 586 us -> 221 us
  local copies, waits for them, and re-layouts: 359 us -> 110 us
  Pallas kernels: 0 us -> 88.5 us
  blocking collectives: 181 us -> 110 us
  matrix products: 65.5 us -> 0.95 us
  starting transfers between devices: 35.6 us -> 14.5 us
  other arithmetic: 32 us -> 16.7 us
    all_to_all x5 -> x1, waiting for transfers between devices: 585 us -> 0.01 us  [body(): x = lax.all_to_all(x, 'expert', split_axis=0, concat_axis=0, tiled=True)]
    ppermute x0 -> x10, waiting for transfers between devices: none -> 166 us  [the longest x8 164 us: halving(): got = lax.ppermute(send, 'expert', [(i, i ^ 1 << b) for i in range(n)])]
    all_to_all x2 -> x1, blocking collectives: 181 us -> 16.5 us  [body(): y = lax.all_to_all(y, 'expert', split_axis=1, concat_axis=1, tiled=True)]
    gather x3 -> x0, local copies, waits for them, and re-layouts: 125 us -> none  [body(): ordered = jnp.take(expert_weights, inverse_order, axis=0)]
    all_gather x0 -> x2, blocking collectives: none -> 93.1 us  [the longest x1 50.6 us: body(): lax.all_gather(route_ids, 'expert', axis=1, tiled=True).reshape(rows, top)]
    pallas_call x0 -> x2, Pallas kernels: none -> 88.5 us  [the longest x1 52.7 us: body(): pl.pallas_call(functools.partial(down_kernel, parts), out_shape=jax.Shape...]
    reshape x11 -> x4, local copies, waits for them, and re-layouts: 116 us -> 50.9 us  [the longest x1 48.4 us: body(): cut = expert_weights.reshape(experts, local, 3, parts, share)]
    dot_general x15 -> x2, matrix products: 65.5 us -> 0.95 us  [dot(): lax.dot_general(a, b, (((ca,), (cb,)), ((), ())), preferred_element_type=...]
  transfers between devices with their start and end apart: 8 -> 12, of which waited for: 4 -> 9; matrix products, arithmetic and copies ran while one was open for 20% -> 5% of each run, Pallas kernels for 0% -> 0%
where the time goes in v1:
time: 576 us; the launch traced here: 575 us
  waiting for transfers between devices  221 us (38%)
  local copies, waits for them, and re-layouts  110 us (19%)
  blocking collectives  110 us (19%)
  Pallas kernels  88.5 us (15%)
  other arithmetic  16.7 us (3%)
  starting transfers between devices  14.5 us (3%)
  between operations  13.8 us (2%)
    ppermute x8, waiting for transfers between devices, halving(): got = lax.ppermute(send, 'expert', [(i, i ^ 1 << b) for i in range(n)])  164 us
    all_gather x1, waiting for transfers between devices, body(): h = lax.all_gather(h, 'expert', axis=0, tiled=True)  54.8 us
    pallas_call x1, Pallas kernels, body(): pl.pallas_call(functools.partial(down_kernel, parts), out_shape=jax.Shape...  52.7 us
    all_gather x1, blocking collectives, body(): lax.all_gather(route_ids, 'expert', axis=1, tiled=True).reshape(rows, top)  50.6 us
    reshape x1, local copies, waits for them, and re-layouts, body(): cut = expert_weights.reshape(experts, local, 3, parts, share)  48.4 us
    all_gather x1, blocking collectives, body(): lax.all_gather(gate_values, 'expert', axis=1, tiled=True).reshape(rows, top)  42.5 us
    pallas_call x1, Pallas kernels, body(): pl.pallas_call(functools.partial(up_kernel, parts), out_shape=jax.ShapeDt...  35.8 us
    dynamic_slice x1, local copies, waits for them, and re-layouts, body(): cut = lax.dynamic_index_in_dim(cut, to, 3, keepdims=False)  25.4 us
  transfers between devices with their start and end apart: 12, of which 9 were waited for; matrix products, arithmetic and copies ran while one was open for 5% of the time, Pallas kernels for 0%

profile of v1, /device:TPU:0, one launch (start us, length us, event | category | flops | bytes accessed | tf_op | source)
XLA Modules:
  0.0 575.4 jit_solution(11118367043305928336)
XLA Ops:
  6.5 48.4 %reshape.137 = bf16[16,224,3,2,512]{4,3,2,1,0:T(2,128)(2,1)} reshape(bf16[16,224,3072]{2,1,0:T(8,128)(2,1)} %refs_0_.3) | data formatting | bytes 44040192 | tf_op jit(solution)/shard_map/reshape | solution.py:140
  54.9 25.4 %constant_dynamic-slice_fusion.4 = bf16[16,224,3,1,512]{4,3,2,1,0:T(2,128)(2,1)S(1)} fusion(bf16[16,224,3,2,512]{4,3,2,1,0:T(2,128)(2,1)} %reshape.137, s32[]{:T(128)S(6)} %select_n.123), kind=kLoop, calls=%fused_computation.60 | loop fusion | bytes 22020100 | tf_op jit(solution)/shard_map/jit(dynamic_index_in_dim)/dynamic_slice | solution.py:141
  80.3 6.1 %copy.78 = bf16[16,224,3,1,512]{4,1,0,2,3:T(8,128)(2,1)} copy(bf16[16,224,3,1,512]{4,3,2,1,0:T(2,128)(2,1)S(1)} %constant_dynamic-slice_fusion.4) | data formatting | bytes 22020096
  86.4 0.5 collective-permute-start
  86.9 1.1 reshape.135
  88.0 1.3 copy.55
  89.3 7.9 %all-to-all-start = ((bf16[16,2,3,16,224]{4,3,2,1,0:T(8,128)(2,1)}), bf16[16,2,3,16,224]{4,3,2,1,0:T(8,128)(2,1)S(1)}, u32[]{:S(2)}, u32[]{:S(2)}) async-start(bf16[16,2,3,16,224]{4,3,2,1,0:T(8,128)(2,1)} %copy.55), calls=%async_computation | async-start | bytes 1572864 | tf_op jit(solution)/shard_map/all_to_all | solution.py:134
  97.3 0.1 copy.51
  97.4 50.6 %all_gather.9 = s32[3,256,8]{2,0,1:T(4,128)S(1)} all-gather(s32[3,16,8]{2,0,1:T(4,128)S(1)} %copy.51), channel_id=1, replica_groups=mesh['fsdp'=2,'expert'=16] {'expert'}, dimensions={1}, use_global_device_ids=true | all-gather | bytes 26112 | tf_op jit(solution)/shard_map/all_gather | solution.py:128
  148.0 0.1 copy.52
  148.2 0.6 convert_reduce_fusion
  148.9 0.6 and_select_fusion
  149.5 0.7 select_reduce_fusion.1
  150.2 0.3 fusion.13
  150.5 0.7 broadcast_in_dim.54.slots_ref
  151.3 1.1 pad_maximum_fusion.x_ref
  152.4 35.8 %shard_map.64 = bf16[2,6528,512]{2,1,0:T(8,128)(2,1)} custom-call(s32[16]{0:T(128)} %copy-done.10, s32[16]{0:T(128)} %get-tuple-element.13.chunks, s32[16]{0:T(128)} %get-tuple-element.17.order, s32[1]{0:T(128)} %bitcast.1.mine, s32[16,1,768]{2,1,0:T(1,128)} %broadcast_in_dim.54.slots_ref, bf16[2,768,224]{2,1,0:T(8,128)(2,1)} %pad_maximum_fusion.x_ref, ...), custom_call_target="tpu_custom_call" | custom-call | flops 5872025600 | bytes 30000000 | tf_op jit(solution)/shard_map/pallas_call | solution.py:167
  188.2 8.3 %fusion.33 = (bf16[1,6400,512]{2,1,0:T(8,128)(2,1)S(1)}, bf16[1,6400,512]{2,1,0:T(8,128)(2,1)}) fusion(bf16[2,6528,512]{2,1,0:T(8,128)(2,1)} %shard_map.64), kind=kLoop, calls=%fused_computation.75 | loop fusion | bytes 26214400 | tf_op jit(solution)/shard_map/slice | solution.py:182
  196.5 0.4 constant_dynamic-slice_fusion.3
  197.0 1.9 copy.80
  198.9 1.6 collective-permute-start.1
  200.4 3.3 constant_dynamic-slice_fusion.1
  203.8 0.3 copy.79
  204.1 0.1 collective-permute-start.5
  204.1 61.2 %collective-permute-done.1 = bf16[2,2,2,400,512]{4,3,1,0,2:T(8,128)(2,1)} collective-permute-done((bf16[2,2,2,400,512]{4,3,1,0,2:T(8,128)(2,1)}, bf16[2,2,2,400,512]{4,3,1,0,2:T(8,128)(2,1)}, u32[]{:S(2)}, u32[]{:S(2)}) %collective-permute-start.1) | collective-permute-done | bytes 3276832 | tf_op jit(solution)/shard_map/ppermute | solution.py:108
  265.4 2.9 convert_add_fusion.1
  268.3 0.2 fusion.4
  268.5 0.1 collective-permute-start.2
  268.6 7.5 %collective-permute-done.5 = bf16[2,2,2,400,512]{4,3,1,0,2:T(8,128)(2,1)S(1)} collective-permute-done((bf16[2,2,2,400,512]{4,3,1,0,2:T(8,128)(2,1)S(1)}, bf16[2,2,2,400,512]{4,3,1,0,2:T(8,128)(2,1)S(1)}, u32[]{:S(2)}, u32[]{:S(2)}) %collective-permute-start.5) | collective-permute-done | bytes 3276832 | tf_op jit(solution)/shard_map/ppermute | solution.py:108
  276.0 1.0 convert_add_fusion
  277.0 1.6 fusion.5
  278.6 1.6 copy-done.1
  280.2 0.1 collective-permute-start.6
  280.3 24.8 %collective-permute-done.2 = bf16[2,2,400,512]{3,2,1,0:T(8,128)(2,1)} collective-permute-done((bf16[2,2,400,512]{3,2,1,0:T(8,128)(2,1)S(1)}, bf16[2,2,400,512]{3,2,1,0:T(8,128)(2,1)}, u32[]{:S(2)}, u32[]{:S(2)}) %collective-permute-start.2) | collective-permute-done | bytes 1638432 | tf_op jit(solution)/shard_map/ppermute | solution.py:108
  305.1 3.1 bitcast_add_fusion.1
  308.2 1.0 fusion.20
  309.2 2.0 bitcast_add_fusion
  311.3 1.7 copy-done.3
  312.9 1.0 fusion.21
  313.9 2.9 collective-permute-start.7
  316.9 40.1 %collective-permute-done.3 = bf16[2,400,512]{2,1,0:T(8,128)(2,1)} collective-permute-done((bf16[2,400,512]{2,1,0:T(8,128)(2,1)}, bf16[2,400,512]{2,1,0:T(8,128)(2,1)}, u32[]{:S(2)}, u32[]{:S(2)}) %collective-permute-start.3) | collective-permute-done | bytes 819232 | tf_op jit(solution)/shard_map/ppermute | solution.py:108
  357.0 1.4 bitcast_add_fusion.3
  358.5 1.3 collective-permute-start.4
  359.7 14.8 %collective-permute-done.7 = bf16[2,400,512]{2,1,0:T(8,128)(2,1)} collective-permute-done((bf16[2,400,512]{2,1,0:T(8,128)(2,1)}, bf16[2,400,512]{2,1,0:T(8,128)(2,1)}, u32[]{:S(2)}, u32[]{:S(2)}) %collective-permute-start.7) | collective-permute-done | bytes 819232 | tf_op jit(solution)/shard_map/ppermute | solution.py:108
  374.5 1.4 bitcast_add_fusion.2
  376.1 0.1 collective-permute-start.8
  376.1 7.1 %collective-permute-done.4 = bf16[400,512]{1,0:T(8,128)(2,1)S(1)} collective-permute-done((bf16[400,512]{1,0:T(8,128)(2,1)S(1)}, bf16[400,512]{1,0:T(8,128)(2,1)S(1)}, u32[]{:S(2)}, u32[]{:S(2)}) %collective-permute-start.4) | collective-permute-done | bytes 409632 | tf_op jit(solution)/shard_map/ppermute | solution.py:108
  383.2 8.7 %collective-permute-done.8 = bf16[400,512]{1,0:T(8,128)(2,1)S(1)} collective-permute-done((bf16[400,512]{1,0:T(8,128)(2,1)S(1)}, bf16[400,512]{1,0:T(8,128)(2,1)S(1)}, u32[]{:S(2)}, u32[]{:S(2)}) %collective-permute-start.8) | collective-permute-done | bytes 409632 | tf_op jit(solution)/shard_map/ppermute | solution.py:108
  391.9 2.2 fusion.23
  394.1 0.1 copy.53
  394.2 42.5 %all_gather.10 = bf16[3,256,8]{2,0,1:T(4,128)(2,1)S(1)} all-gather(bf16[3,16,8]{2,0,1:T(4,128)(2,1)S(1)} %copy.53), channel_id=1, replica_groups=mesh['fsdp'=2,'expert'=16] {'expert'}, dimensions={1}, use_global_device_ids=true | all-gather | bytes 13056 | tf_op jit(solution)/shard_map/all_gather | solution.py:129
  436.7 0.1 copy.54
  436.9 0.6 broadcast_in_dim.57.gates_ref
  437.6 54.8 %all-gather.2.cloned.1.call-done.h_ref = bf16[6400,512]{1,0:T(8,128)(2,1)} async-done(((bf16[400,512]{1,0:T(8,128)(2,1)}), bf16[6400,512]{1,0:T(8,128)(2,1)}) %all-gather.2.cloned.1.call-update) | async-done | bytes 6553616 | tf_op jit(solution)/shard_map/all_gather | solution.py:185
  492.4 52.7 %shard_map.65 = f32[2,768,224]{2,1,0:T(8,128)} custom-call(s32[16]{0:T(128)} %copy-done.10, s32[16]{0:T(128)} %get-tuple-element.13.chunks, s32[16]{0:T(128)} %get-tuple-element.17.order, s32[1]{0:T(128)} %bitcast.1.mine, s32[16,1,768]{2,1,0:T(1,128)} %broadcast_in_dim.54.slots_ref, f32[16,1,768]{2,1,0:T(1,128)} %broadcast_in_dim.57.gates_ref, ...), custom_call_target="tpu_custom_call" | custom-call | flops 11744051200 | bytes 20000000 | tf_op jit(solution)/shard_map/pallas_call | solution.py:187
  545.1 1.3 slice_bitcast_fusion
  546.4 0.3 copy.62
  546.7 0.1 collective-permute-start.9
  546.8 2.3 collective-permute-done.9
  549.0 1.4 copy.63
  550.4 0.1 fusion.25
  550.6 16.5 %all_to_all.10 = bf16[3,16,16,224]{3,2,0,1:T(8,128)(2,1)S(1)} all-to-all(bf16[3,16,16,224]{3,2,0,1:T(8,128)(2,1)S(1)} %copy.64), channel_id=1, replica_groups=mesh['fsdp'=2,'expert'=16] {'expert'}, dimensions={1} | all-to-all | bytes 688128 | tf_op jit(solution)/shard_map/all_to_all | solution.py:204
  567.1 0.1 copy.65
  567.2 1.3 reshape.139
  (39 shorter events, 0.5 us)
Async XLA Ops:
  80.3 6.6 %copy-start.7 = (bf16[3,16,7168]{2,1,0:T(8,128)(2,1)S(1)}, bf16[3,16,7168]{2,1,0:T(8,128)(2,1)}, u32[]{:S(2)}) copy-start(bf16[3,16,7168]{2,1,0:T(8,128)(2,1)} %param.6) | copy-start | bytes 2064388
  86.4 10.8 %copy-start.8 = (s32[3,16,8]{1,2,0:T(8,128)S(1)}, s32[3,16,8]{1,2,0:T(8,128)}, u32[]{:S(2)}) copy-start(s32[3,16,8]{1,2,0:T(8,128)} %param.7) | copy-start | bytes 4612
  86.4 61.8 %copy-start.12 = (s32[16]{0:T(128)S(1)}, s32[16]{0:T(128)}, u32[]{:S(2)}) copy-start(s32[16]{0:T(128)} %param.9) | copy-start | bytes 196
  86.4 66.0 %collective-permute-start = (bf16[3,16,224,512]{3,2,1,0:T(8,128)(2,1)}, bf16[3,16,224,512]{3,2,1,0:T(8,128)(2,1)}, u32[]{:S(2)}, u32[]{:S(2)}) collective-permute-start(bf16[3,16,224,512]{3,2,1,0:T(8,128)(2,1)} %bitcast.74), channel_id=1, source_target_pairs={{0,16},{16,0},{1,17},{17,1},{2,18},{18,2},{3,19},{19,3},{4,20},{20... | collective-permute-start | bytes 33030152 | tf_op jit(solution)/shard_map/ppermute | solution.py:143
  88.0 61.5 %copy-start.11 = (s32[16]{0:T(128)S(1)}, s32[16]{0:T(128)}, u32[]{:S(2)}) copy-start(s32[16]{0:T(128)} %param.10) | copy-start | bytes 196
  89.3 61.8 %all-to-all-start = ((bf16[16,2,3,16,224]{4,3,2,1,0:T(8,128)(2,1)}), bf16[16,2,3,16,224]{4,3,2,1,0:T(8,128)(2,1)S(1)}, u32[]{:S(2)}, u32[]{:S(2)}) async-start(bf16[16,2,3,16,224]{4,3,2,1,0:T(8,128)(2,1)} %copy.55), calls=%async_computation | async-start | bytes 1572864 | tf_op jit(solution)/shard_map/all_to_all | solution.py:134
  97.2 395.2 %all-gather.2.cloned.1.call-start = ((), (), s32[]{:S(2)}) async-start(), calls=%async_computation.2 | async-start | bytes 6963200 | tf_op jit(solution)/shard_map/all_gather | solution.py:185
  150.2 2.3 copy-start.10
  198.9 66.5 %collective-permute-start.1 = (bf16[2,2,2,400,512]{4,3,1,0,2:T(8,128)(2,1)}, bf16[2,2,2,400,512]{4,3,1,0,2:T(8,128)(2,1)}, u32[]{:S(2)}, u32[]{:S(2)}) collective-permute-start(bf16[2,2,2,400,512]{4,3,1,0,2:T(8,128)(2,1)} %bitcast.76), channel_id=1, source_target_pairs={{0,1},{1,0},{2,3},{3,2},{4,5},{5,4},{6,7},{7,6},{8,9},{9,8},{10,11... | collective-permute-start | bytes 9830408 | tf_op jit(solution)/shard_map/ppermute | solution.py:108
  204.1 72.0 %collective-permute-start.5 = (bf16[2,2,2,400,512]{4,3,1,0,2:T(8,128)(2,1)S(1)}, bf16[2,2,2,400,512]{4,3,1,0,2:T(8,128)(2,1)S(1)}, u32[]{:S(2)}, u32[]{:S(2)}) collective-permute-start(bf16[2,2,2,400,512]{4,3,1,0,2:T(8,128)(2,1)S(1)} %bitcast.79), channel_id=1, source_target_pairs={{0,2},{1,3},{2,0},{3,1},{4,6},{5,7},{6,4},{7,5},{8,10},{9,11},{10,... | collective-permute-start | bytes 9830408 | tf_op jit(solution)/shard_map/ppermute | solution.py:108
  268.3 8.7 %copy-start = (f32[2,2,2,400,512]{4,3,1,0,2:T(8,128)}, f32[2,2,2,400,512]{4,3,1,0,2:T(8,128)S(1)}, u32[]{:S(2)}) copy-start(f32[2,2,2,400,512]{4,3,1,0,2:T(8,128)S(1)} %convert_add_fusion.1) | copy-start | bytes 19660804
  268.5 36.6 %collective-permute-start.2 = (bf16[2,2,400,512]{3,2,1,0:T(8,128)(2,1)S(1)}, bf16[2,2,400,512]{3,2,1,0:T(8,128)(2,1)}, u32[]{:S(2)}, u32[]{:S(2)}) collective-permute-start(bf16[2,2,400,512]{3,2,1,0:T(8,128)(2,1)S(1)} %fusion.4), channel_id=1, source_target_pairs={{0,2},{1,3},{2,0},{3,1},{4,6},{5,7},{6,4},{7,5},{8,10},{9,11},{10,... | collective-permute-start | bytes 4915208 | tf_op jit(solution)/shard_map/ppermute | solution.py:108
  277.0 3.2 copy-start.1
  280.2 29.0 %collective-permute-start.6 = (bf16[2,2,400,512]{3,2,1,0:T(8,128)(2,1)}, bf16[2,2,400,512]{3,2,1,0:T(8,128)(2,1)}, u32[]{:S(2)}, u32[]{:S(2)}) collective-permute-start(bf16[2,2,400,512]{3,2,1,0:T(8,128)(2,1)} %fusion.5), channel_id=1, source_target_pairs={{0,1},{1,0},{2,3},{3,2},{4,5},{5,4},{6,7},{7,6},{8,9},{9,8},{10,11... | collective-permute-start | bytes 4915208 | tf_op jit(solution)/shard_map/ppermute | solution.py:108
  280.3 28.9 %copy-start.2 = (f32[2,2,2,400,512]{4,3,1,0,2:T(8,128)S(1)}, f32[2,2,2,400,512]{4,3,1,0,2:T(8,128)}, u32[]{:S(2)}) copy-start(f32[2,2,2,400,512]{4,3,1,0,2:T(8,128)} %copy-done.1) | copy-start | bytes 19660804
  309.2 47.7 %collective-permute-start.3 = (bf16[2,400,512]{2,1,0:T(8,128)(2,1)}, bf16[2,400,512]{2,1,0:T(8,128)(2,1)}, u32[]{:S(2)}, u32[]{:S(2)}) collective-permute-start(bf16[2,400,512]{2,1,0:T(8,128)(2,1)} %fusion.20), channel_id=1, source_target_pairs={{0,8},{1,9},{2,10},{3,11},{4,12},{5,13},{6,14},{7,15},{8,0},{9,1},... | collective-permute-start | bytes 2457608 | tf_op jit(solution)/shard_map/ppermute | solution.py:108
  311.2 1.7 copy-start.3
  313.9 60.6 %collective-permute-start.7 = (bf16[2,400,512]{2,1,0:T(8,128)(2,1)}, bf16[2,400,512]{2,1,0:T(8,128)(2,1)}, u32[]{:S(2)}, u32[]{:S(2)}) collective-permute-start(bf16[2,400,512]{2,1,0:T(8,128)(2,1)} %fusion.21), channel_id=1, source_target_pairs={{0,8},{1,9},{2,10},{3,11},{4,12},{5,13},{6,14},{7,15},{8,0},{9,1},... | collective-permute-start | bytes 2457608 | tf_op jit(solution)/shard_map/ppermute | solution.py:108
  316.9 57.7 %copy-start.4 = (f32[2,2,400,512]{3,2,1,0:T(8,128)S(1)}, f32[2,2,400,512]{3,2,1,0:T(8,128)}, u32[]{:S(2)}) copy-start(f32[2,2,400,512]{3,2,1,0:T(8,128)} %copy-done.3) | copy-start | bytes 9830404
  358.4 17.6 %copy-start.5 = (f32[2,400,512]{2,1,0:T(8,128)}, f32[2,400,512]{2,1,0:T(8,128)S(1)}, u32[]{:S(2)}) copy-start(f32[2,400,512]{2,1,0:T(8,128)S(1)} %bitcast_add_fusion.3) | copy-start | bytes 4915204
  358.5 35.7 %copy-start.9 = (bf16[3,16,8]{1,2,0:T(8,128)(2,1)S(1)}, bf16[3,16,8]{1,2,0:T(8,128)(2,1)}, u32[]{:S(2)}) copy-start(bf16[3,16,8]{1,2,0:T(8,128)(2,1)} %param.8) | copy-start | bytes 2308
  358.5 24.7 %collective-permute-start.4 = (bf16[400,512]{1,0:T(8,128)(2,1)S(1)}, bf16[400,512]{1,0:T(8,128)(2,1)S(1)}, u32[]{:S(2)}, u32[]{:S(2)}) collective-permute-start(bf16[400,512]{1,0:T(8,128)(2,1)S(1)} %fusion.26), channel_id=1, source_target_pairs={{0,4},{1,5},{2,6},{3,7},{4,0},{5,1},{6,2},{7,3},{8,12},{9,13},{10,... | collective-permute-start | bytes 1228808 | tf_op jit(solution)/shard_map/ppermute | solution.py:108
  376.1 15.8 %collective-permute-start.8 = (bf16[400,512]{1,0:T(8,128)(2,1)S(1)}, bf16[400,512]{1,0:T(8,128)(2,1)S(1)}, u32[]{:S(2)}, u32[]{:S(2)}) collective-permute-start(bf16[400,512]{1,0:T(8,128)(2,1)S(1)} %fusion.27), channel_id=1, source_target_pairs={{0,4},{1,5},{2,6},{3,7},{4,0},{5,1},{6,2},{7,3},{8,12},{9,13},{10,... | collective-permute-start | bytes 1228808 | tf_op jit(solution)/shard_map/ppermute | solution.py:108
  545.1 5.3 copy-start.6
  546.7 2.3 collective-permute-start.9
Sparse Core Ops, SparseCore 0:
  394.2 98.1 all-gather.1

commit v2 on v1

v2 whole, which is shorter than its diff:
```python
import functools

import jax
import jax.numpy as jnp
from jax import lax
from jax.experimental import pallas as pl
from jax.experimental.pallas import tpu as pltpu
from jax.sharding import PartitionSpec as P

TILE = 128
HALVES = 2
ALIGN = 16
BF16 = jnp.bfloat16
F32 = jnp.float32


def dot(a, b, ca=1, cb=0):
    return lax.dot_general(a, b, (((ca,), (cb,)), ((), ())), preferred_element_type=F32)


def tables(route_ids, gate_values, cap_limit, block_rows):
    rows = route_ids.shape[0]
    experts = cap_limit.shape[0]
    hot = route_ids[:, :, None] == jnp.arange(experts, dtype=jnp.int32)[None, None, :]
    chosen = jnp.any(hot, axis=1)
    gates = jnp.sum(jnp.where(hot, gate_values[:, :, None].astype(F32), 0.0), axis=1)
    at = jnp.arange(rows, dtype=jnp.int32)
    earlier = at[None, :] < at[:, None]
    same = at[None, :] // block_rows == at[:, None] // block_rows
    position = dot((earlier & same).astype(BF16), chosen.astype(BF16)).astype(jnp.int32)
    kept = chosen & (position < cap_limit[None, :])
    before = dot(earlier.astype(BF16), kept.astype(BF16)).astype(jnp.int32)
    counts = jnp.sum(kept.astype(jnp.int32), axis=0)
    padded = (counts + (ALIGN - 1)) // ALIGN * ALIGN
    es = jnp.arange(experts, dtype=jnp.int32)
    starts = jnp.sum(jnp.where(es[None, :] < es[:, None], padded[None, :], 0), axis=1)
    slots = jnp.where(kept, before + starts[None, :], -1)
    chunks = (counts + (TILE - 1)) // TILE
    return slots.T[:, None, :], gates.T[:, None, :], starts, chunks


def up_kernel(parts, fresh, starts, chunks, order, mine, *refs):
    if fresh:
        slots_ref, x_ref, weights, (out_ref, packed_ref) = refs[0], refs[1], refs[2:-2], refs[-2:]
    else:
        packed_ref, weights, out_ref = refs[0], refs[1:-1], refs[-1]
    e = pl.program_id(0)

    @pl.when(e == 0)
    def _():
        out_ref[...] = jnp.zeros_like(out_ref)

    def step(c, carry):
        base = pl.multiple_of(starts[e] + c * TILE, ALIGN)
        if fresh:
            slots = slots_ref[0]
            pick = slots == base + lax.broadcasted_iota(jnp.int32, (TILE, slots.shape[1]), 0)
            pick = pick.astype(F32).astype(BF16)
        a = b = None
        for i in range(parts):
            if fresh:
                xs = dot(pick, x_ref[i]).astype(BF16)
                packed_ref[i, pl.ds(base, TILE), :] = xs
            else:
                xs = packed_ref[i, pl.ds(base, TILE), :]
            da = dot(xs, weights[2 * i][0])
            db = dot(xs, weights[2 * i + 1][0])
            a, b = (da, db) if a is None else (a + da, b + db)
        out_ref[0, pl.ds(base, TILE), :] = a.astype(out_ref.dtype)
        out_ref[1, pl.ds(base, TILE), :] = b.astype(out_ref.dtype)
        return carry

    lax.fori_loop(0, chunks[e], step, 0)


def down_kernel(parts, starts, chunks, order, mine, slots_ref, gates_ref, *refs):
    h_refs, weights, out_ref = refs[:HALVES], refs[HALVES:-1], refs[-1]
    e = pl.program_id(0)
    total, cols = h_refs[0].shape

    @pl.when(e == 0)
    def _():
        out_ref[...] = jnp.zeros_like(out_ref)

    slots = slots_ref[0]
    gates = gates_ref[0]

    def step(c, carry):
        first = starts[e] + c * TILE
        base = pl.multiple_of(jnp.minimum(first, total - TILE), ALIGN)
        number = base + lax.broadcasted_iota(jnp.int32, (TILE, slots.shape[1]), 0)
        mix = jnp.where((slots == number) & (number >= first), gates, 0.0).astype(BF16)
        h = [h_ref[pl.ds(base, TILE), :] for h_ref in h_refs]
        for i in range(parts):
            y = sum(dot(h[q], weights[i][0, :, q * cols : (q + 1) * cols], 1, 1) for q in range(HALVES))
            high = y.astype(BF16)
            low = (y - high.astype(F32)).astype(BF16)
            out_ref[i] += dot(mix, high, 0, 0) + dot(mix, low, 0, 0)
        return carry

    lax.fori_loop(0, chunks[e], step, 0)


def halve(cur, left, b, n):
    axis = left.index(b)
    bit = (lax.axis_index("expert") >> b) & 1
    send = lax.dynamic_index_in_dim(cur, 1 - bit, axis, keepdims=False).astype(BF16)
    keep = lax.dynamic_index_in_dim(cur, bit, axis, keepdims=False).astype(F32)
    got = lax.ppermute(send, "expert", [(i, i ^ (1 << b)) for i in range(n)])
    return keep + got.astype(F32), [i for i in left if i != b]


def reduce_all(pieces, n):
    bits = n.bit_length() - 1
    later = list(range(bits - 1, 1, -1))
    orders = ([0, 1] + later, [1, 0] + later)
    left = list(range(bits - 1, -1, -1))
    state = [[(i.reshape((2,) * bits + (i.shape[0] // n, i.shape[1])), left) for i in pair] for pair in pieces]
    done = [None] * len(state)
    for turn in range(bits + 2 * (len(state) - 1)):
        for q in range(len(state)):
            at = turn - 2 * q
            if 0 <= at < bits:
                state[q] = [halve(*state[q][k], orders[k][at], n) for k in range(2)]
        held = lax.optimization_barrier([[i for i, _ in pair] for pair in state])
        state = [[(i, pair[k][1]) for k, i in enumerate(new)] for new, pair in zip(held, state)]
        for q in range(len(state)):
            if turn - 2 * q == bits - 1:
                a, b = (i for i, _ in state[q])
                done[q] = lax.all_gather((a * jax.nn.sigmoid(a) * b).astype(BF16), "expert", axis=0, tiled=True)
    return done


def body(tokens, route_ids, gate_values, cap_limit, update_ids, expert_weights):
    steps, block_rows, width = tokens.shape
    top = route_ids.shape[2]
    experts = cap_limit.shape[0]
    parts = lax.axis_size("fsdp")
    owners = lax.axis_size("expert")
    local = expert_weights.shape[1]
    hidden = expert_weights.shape[2] // 3
    share = hidden // parts
    rows = steps * owners * block_rows
    f = lax.axis_index("fsdp")

    es = jnp.arange(experts, dtype=jnp.int32)
    order = jnp.sum(jnp.where(update_ids[None, :] == es[:, None], es[None, :], 0), axis=1)

    others = []
    for s in range(1, parts):
        to = (f + s) % parts
        pairs = [(i, (i + s) % parts) for i in range(parts)]
        cuts = [
            lax.dynamic_slice(expert_weights, (0, 0, kind * hidden + to * share), (experts, local, share))
            for kind in range(3)
        ]
        others.append([lax.ppermute(cut, "fsdp", pairs) for cut in cuts])

    x = tokens.reshape(steps, block_rows, parts, owners, local)
    x = jnp.transpose(x, (3, 0, 1, 2, 4)).reshape(owners, steps, block_rows, parts * local)
    routes = jnp.concatenate([route_ids.astype(BF16), gate_values], axis=2)
    routes = jnp.broadcast_to(routes[None], (owners,) + routes.shape)
    x = jnp.concatenate([x, routes], axis=3)
    x = lax.all_to_all(x, "expert", split_axis=0, concat_axis=0, tiled=True)
    x = jnp.transpose(x, (1, 0, 2, 3)).reshape(rows, parts * local + 2 * top)
    ids = x[:, parts * local : parts * local + top].astype(jnp.int32)
    gate = x[:, parts * local + top :]
    slots, gates, starts, chunks = tables(ids, gate, cap_limit, block_rows)
    sources = [(f - s) % parts for s in range(parts)]
    x = jnp.stack([lax.dynamic_slice(x, (0, i * local), (rows, local)) for i in sources])

    packed = -(-(rows * top + experts * (ALIGN - 1)) // (ALIGN * owners)) * ALIGN * owners
    mine = f.astype(jnp.int32).reshape(1)
    whole = lambda *shape: pl.BlockSpec(shape, lambda e, *_: (0,) * len(shape))
    line = pl.BlockSpec((1, 1, rows), lambda e, *_: (e, 0, 0))

    def own(kind, cols, q):
        return pl.BlockSpec((1, local, cols), lambda e, st, ch, od, mi: (od[e], 0, (kind * parts + mi[0]) * (share // cols) + q))

    def other(cols, q):
        return pl.BlockSpec((1, local, cols), lambda e, st, ch, od, mi: (od[e], 0, q))

    scalars = (starts, chunks, order, mine)
    params = pltpu.CompilerParams(vmem_limit_bytes=58 * 2**20)
    cols = share // HALVES
    xs = None
    pieces = []
    for q in range(HALVES):
        specs, args = [own(0, cols, q), own(1, cols, q)], [expert_weights] * 2
        for got in others:
            specs += [other(cols, q)] * 2
            args += got[:2]
        ab_shape = (2, packed + TILE, cols)
        xs_shape = (parts, packed + TILE, local)
        fresh = q == 0
        made = pl.pallas_call(
            functools.partial(up_kernel, parts, fresh),
            out_shape=[jax.ShapeDtypeStruct(i, BF16) for i in ([ab_shape, xs_shape] if fresh else [ab_shape])],
            grid_spec=pltpu.PrefetchScalarGridSpec(
                num_scalar_prefetch=4,
                grid=(experts,),
                in_specs=([line, whole(parts, rows, local)] if fresh else [whole(*xs_shape)]) + specs,
                out_specs=[whole(*i) for i in ([ab_shape, xs_shape] if fresh else [ab_shape])],
            ),
            compiler_params=params,
            cost_estimate=pl.CostEstimate(flops=2 * 10**10, bytes_accessed=5 * 10**7, transcendentals=0),
        )(*scalars, *([slots, x] if fresh else [xs]), *args)
        if fresh:
            xs = made[1]
        ab = made[0]
        pieces.append([ab[0, :packed], ab[1, :packed]])
    hs = reduce_all(pieces, owners)
    down_specs, down_args = [own(2, share, 0)], [expert_weights]
    for got in others:
        down_specs.append(other(share, 0))
        down_args.append(got[2])

    out = pl.pallas_call(
        functools.partial(down_kernel, parts),
        out_shape=jax.ShapeDtypeStruct((parts, rows, local), F32),
        grid_spec=pltpu.PrefetchScalarGridSpec(
            num_scalar_prefetch=4,
            grid=(experts,),
            in_specs=[line, line, *[whole(packed, cols)] * HALVES] + down_specs,
            out_specs=whole(parts, rows, local),
        ),
        compiler_params=params,
        cost_estimate=pl.CostEstimate(flops=2 * packed * local * parts * (share + 2 * rows), bytes_accessed=2 * 10**7, transcendentals=0),
    )(*scalars, slots, gates, *hs, *down_args)

    total = lax.dynamic_index_in_dim(out, 0, 0, keepdims=False)
    for s in range(1, parts):
        total = total + lax.ppermute(out[s], "fsdp", [(i, (i - s) % parts) for i in range(parts)])
    y = total.astype(BF16).reshape(steps, owners, block_rows, local)
    y = lax.all_to_all(y, "expert", split_axis=1, concat_axis=1, tiled=True)
    return jnp.transpose(y, (0, 2, 1, 3)).reshape(steps, block_rows, owners * local)


def solution(mesh):
    return jax.shard_map(
        body,
        mesh=mesh,
        in_specs=(
            P(None, "expert", None),
            P(None, "expert", None),
            P(None, "expert", None),
            P(),
            P(),
            P(None, ("fsdp", "expert"), None),
        ),
        out_specs=P(None, "expert", "fsdp"),
        check_vma=False,
    )
```

time: 576 us -> 460 us (0.80)
  blocking collectives: 110 us -> 16.8 us
  local copies, waits for them, and re-layouts: 110 us -> 35.7 us
  waiting for transfers between devices: 221 us -> 242 us
  starting transfers between devices: 14.5 us -> 31.5 us
  Pallas kernels: 88.5 us -> 98.1 us
    all_gather x2 -> x0, blocking collectives: 93.1 us -> none  [the longest x1 50.6 us: body(): lax.all_gather(route_ids, 'expert', axis=1, tiled=True).reshape(rows, top)]
    reshape x1, local copies, waits for them, and re-layouts: 48.4 us -> 0.42 us  [body(): jnp.transpose(x, (3, 0, 1, 2, 4))]
    all_gather x1 -> x2, waiting for transfers between devices: 54.8 us -> 95.2 us  [reduce_all(): lax.all_gather((a * jax.nn.sigmoid(a) * b).astype(BF16), 'expert', axis=0...]
    ppermute x9 -> x19, waiting for transfers between devices: 164 us -> 125 us  [the longest x16 119 us: halve(): got = lax.ppermute(send, 'expert', [(i, i ^ 1 << b) for i in range(n)])]
    all_to_all x1, waiting for transfers between devices: 0.01 us -> 19.6 us  [body(): x = lax.all_to_all(x, 'expert', split_axis=0, concat_axis=0, tiled=True)]
    dynamic_slice x6 -> x5, local copies, waits for them, and re-layouts: 31.4 us -> 13 us  [the longest x1 8.69 us: body(): lax.dynamic_slice(expert_weights, (0, 0, kind * hidden + to * share), (ex...]
    ppermute x9 -> x19, starting transfers between devices: 6.49 us -> 22.7 us  [the longest x16 22.1 us: halve(): got = lax.ppermute(send, 'expert', [(i, i ^ 1 << b) for i in range(n)])]
    pallas_call x1 -> x2, Pallas kernels: 35.8 us -> 49.9 us  [body(): pl.pallas_call(functools.partial(up_kernel, parts, fresh), out_shape=[jax...]
  transfers between devices with their start and end apart: 12 -> 23, of which waited for: 9 -> 19; matrix products, arithmetic and copies ran while one was open for 5% -> 7% of each run, Pallas kernels for 0% -> 5%
where the time goes in v2:
time: 460 us; the launch traced here: 457 us
  waiting for transfers between devices  242 us (53%)
  Pallas kernels  98.1 us (21%)
  local copies, waits for them, and re-layouts  35.7 us (8%)
  starting transfers between devices  31.5 us (7%)
  other arithmetic  18.7 us (4%)
  blocking collectives  16.8 us (4%)
  between operations  13.9 us (3%)
    ppermute x16, waiting for transfers between devices, halve(): got = lax.ppermute(send, 'expert', [(i, i ^ 1 << b) for i in range(n)])  119 us
    all_gather x2, waiting for transfers between devices, reduce_all(): lax.all_gather((a * jax.nn.sigmoid(a) * b).astype(BF16), 'expert', axis=0...  95.2 us
    pallas_call x2, Pallas kernels, body(): pl.pallas_call(functools.partial(up_kernel, parts, fresh), out_shape=[jax...  49.9 us
    pallas_call x1, Pallas kernels, body(): pl.pallas_call(functools.partial(down_kernel, parts), out_shape=jax.Shape...  48.2 us
    ppermute x16, starting transfers between devices, halve(): got = lax.ppermute(send, 'expert', [(i, i ^ 1 << b) for i in range(n)])  22.1 us
    all_to_all x1, waiting for transfers between devices, body(): x = lax.all_to_all(x, 'expert', split_axis=0, concat_axis=0, tiled=True)  19.6 us
    all_to_all x1, blocking collectives, body(): y = lax.all_to_all(y, 'expert', split_axis=1, concat_axis=1, tiled=True)  16.8 us
    add x16, other arithmetic, halve(): return (keep + got.astype(F32), [i for i in left if i != b])  13.3 us
  transfers between devices with their start and end apart: 23, of which 19 were waited for; matrix products, arithmetic and copies ran while one was open for 7% of the time, Pallas kernels for 5%

profile of v2, /device:TPU:0, one launch (start us, length us, event | category | flops | bytes accessed | tf_op | source)
XLA Modules:
  0.0 457.3 jit_solution(2290972678450339463)
XLA Ops:
  6.5 8.7 %constant_dynamic-slice_fusion = (bf16[16,224,512]{2,1,0:T(8,128)(2,1)}, bf16[16,224,512]{2,1,0:T(8,128)(2,1)}, bf16[16,224,512]{2,1,0:T(8,128)(2,1)}) fusion(bf16[16,224,3072]{2,1,0:T(8,128)(2,1)} %refs_2_.5, s32[]{:T(128)S(6)} %select_n.153, s32[]{:T(128)S(6)} %select_n.144, s32[]{:T(128)S(6)} %select_n.143), kind=kLoop, calls=%fused_computation.74 | loop fusion | bytes 22020108 | tf_op jit(solution)/shard_map/dynamic_slice | solution.py:154
  15.9 1.1 reshape.138
  17.0 0.9 copy.116
  18.3 1.1 pad_maximum_fusion
  19.4 8.4 %all-to-all-start = ((bf16[16,3,16,464]{3,2,1,0:T(8,128)(2,1)}), bf16[16,3,16,464]{3,2,1,0:T(8,128)(2,1)S(1)}, u32[]{:S(2)}, u32[]{:S(2)}) async-start(bf16[16,3,16,464]{3,2,1,0:T(8,128)(2,1)} %pad_maximum_fusion), calls=%async_computation | async-start | bytes 1572864 | tf_op jit(solution)/shard_map/all_to_all | solution.py:164
  28.2 19.6 %all-to-all-done = bf16[16,3,16,464]{3,2,1,0:T(8,128)(2,1)S(1)} async-done(((bf16[16,3,16,464]{3,2,1,0:T(8,128)(2,1)}), bf16[16,3,16,464]{3,2,1,0:T(8,128)(2,1)S(1)}, u32[]{:S(2)}, u32[]{:S(2)}) %all-to-all-start) | async-done | bytes 712736 | tf_op jit(solution)/shard_map/all_to_all | solution.py:164
  49.4 0.7 select_reduce_fusion.1
  51.3 1.1 pad_maximum_fusion.1.refs_1_
  52.5 28.7 %shard_map.64 = (bf16[2,6528,256]{2,1,0:T(8,128)(2,1)}, bf16[2,6528,224]{2,1,0:T(8,128)(2,1)}) custom-call(s32[16]{0:T(128)} %copy-done.8, s32[16]{0:T(128)} %get-tuple-element.64.chunks, s32[16]{0:T(128)} %get-tuple-element.68.order, s32[1]{0:T(128)} %bitcast.3.mine, s32[16,1,768]{2,1,0:T(1,128)} %broadcast_in_dim.63.refs_0_.slots_ref, ...), custom_call_target="tpu_custom_call" | custom-call | flops 20000000000 | bytes 50000000 | tf_op jit(solution)/shard_map/pallas_call | solution.py:196
  81.1 3.3 fusion.38
  84.7 1.3 copy.115
  86.6 1.5 constant_dynamic-slice_fusion.4
  88.1 1.3 copy.114
  89.4 1.6 collective-permute-start.3
  91.0 21.2 %shard_map.65 = bf16[2,6528,256]{2,1,0:T(8,128)(2,1)} custom-call(s32[16]{0:T(128)} %copy-done.8, s32[16]{0:T(128)} %get-tuple-element.64.chunks, s32[16]{0:T(128)} %get-tuple-element.68.order, s32[1]{0:T(128)} %bitcast.3.mine, bf16[2,6528,224]{2,1,0:T(8,128)(2,1)} %get-tuple-element.28.refs_0_, bf16[16,224,3072]{2,1,0:T(8,128)(2,1)} %refs_2_.5, ...), custom_call_target="tpu_custom_call" | custom-call | flops 20000000000 | bytes 50000000 | tf_op jit(solution)/shard_map/pallas_call | solution.py:196
  112.2 3.3 fusion.37
  115.6 5.4 %collective-permute-done.2 = bf16[2,2,2,400,256]{4,3,1,0,2:T(8,128)(2,1)} collective-permute-done((bf16[2,2,2,400,256]{4,3,1,0,2:T(8,128)(2,1)}, bf16[2,2,2,400,256]{4,3,1,0,2:T(8,128)(2,1)}, u32[]{:S(2)}, u32[]{:S(2)}) %collective-permute-start.2) | collective-permute-done | bytes 1638432 | tf_op jit(solution)/shard_map/ppermute | solution.py:109
  121.0 1.9 convert_add_fusion.3
  122.9 1.8 collective-permute-done.3
  124.8 1.8 convert_add_fusion.2
  126.6 1.8 collective-permute-start.4
  128.5 1.5 collective-permute-start.5
  130.0 13.4 %collective-permute-done.4 = bf16[2,2,400,256]{3,2,1,0:T(8,128)(2,1)S(1)} collective-permute-done((bf16[2,2,400,256]{3,2,1,0:T(8,128)(2,1)S(1)}, bf16[2,2,400,256]{3,2,1,0:T(8,128)(2,1)S(1)}, u32[]{:S(2)}, u32[]{:S(2)}) %collective-permute-start.4) | collective-permute-done | bytes 819232 | tf_op jit(solution)/shard_map/ppermute | solution.py:109
  143.4 1.4 bitcast_add_fusion.3
  145.0 1.3 bitcast_add_fusion.2
  146.4 1.3 copy_bitcast_fusion.3
  147.7 1.4 collective-permute-start.8
  149.1 1.3 copy_bitcast_fusion.2
  150.4 1.5 collective-permute-start.9
  152.0 2.0 fusion.24
  153.9 3.4 collective-permute-start.6
  157.3 2.0 fusion.25
  159.3 24.2 %collective-permute-done.6 = bf16[2,400,256]{2,1,0:T(8,128)(2,1)} collective-permute-done((bf16[2,400,256]{2,1,0:T(8,128)(2,1)}, bf16[2,400,256]{2,1,0:T(8,128)(2,1)}, u32[]{:S(2)}, u32[]{:S(2)}) %collective-permute-start.6) | collective-permute-done | bytes 409632 | tf_op jit(solution)/shard_map/ppermute | solution.py:109
  183.4 1.4 bitcast_add_fusion.7
  184.8 5.4 %collective-permute-done.7 = bf16[2,400,256]{2,1,0:T(8,128)(2,1)} collective-permute-done((bf16[2,400,256]{2,1,0:T(8,128)(2,1)}, bf16[2,400,256]{2,1,0:T(8,128)(2,1)}, u32[]{:S(2)}, u32[]{:S(2)}) %collective-permute-start.7) | collective-permute-done | bytes 409632 | tf_op jit(solution)/shard_map/ppermute | solution.py:109
  190.2 1.4 bitcast_add_fusion.6
  191.5 1.8 convert_add_fusion.1
  193.3 1.8 convert_add_fusion
  195.2 1.5 collective-permute-start.12
  197.0 1.3 collective-permute-start.13
  198.3 2.1 collective-permute-start.11
  200.4 4.5 collective-permute-done.10
  204.9 2.3 collective-permute-done.11
  207.2 7.2 %collective-permute-done.12 = bf16[2,2,400,256]{3,2,1,0:T(8,128)(2,1)S(1)} collective-permute-done((bf16[2,2,400,256]{3,2,1,0:T(8,128)(2,1)S(1)}, bf16[2,2,400,256]{3,2,1,0:T(8,128)(2,1)S(1)}, u32[]{:S(2)}, u32[]{:S(2)}) %collective-permute-start.12) | collective-permute-done | bytes 819232 | tf_op jit(solution)/shard_map/ppermute | solution.py:109
  214.6 1.9 collective-permute-done.13
  216.6 0.8 multiply_convert_fusion.1
  217.6 1.8 collective-permute-start.14
  219.4 1.3 collective-permute-start.15
  220.7 30.6 %collective-permute-done.14 = bf16[2,400,256]{2,1,0:T(8,128)(2,1)S(1)} collective-permute-done((bf16[2,400,256]{2,1,0:T(8,128)(2,1)S(1)}, bf16[2,400,256]{2,1,0:T(8,128)(2,1)S(1)}, u32[]{:S(2)}, u32[]{:S(2)}) %collective-permute-start.14) | collective-permute-done | bytes 409632 | tf_op jit(solution)/shard_map/ppermute | solution.py:109
  251.4 7.7 %collective-permute-done.15 = bf16[2,400,256]{2,1,0:T(8,128)(2,1)S(1)} collective-permute-done((bf16[2,400,256]{2,1,0:T(8,128)(2,1)S(1)}, bf16[2,400,256]{2,1,0:T(8,128)(2,1)S(1)}, u32[]{:S(2)}, u32[]{:S(2)}) %collective-permute-start.15) | collective-permute-done | bytes 409632 | tf_op jit(solution)/shard_map/ppermute | solution.py:109
  259.3 2.1 collective-permute-start.17
  261.3 8.8 %collective-permute-done.16 = bf16[400,256]{1,0:T(8,128)(2,1)S(1)} collective-permute-done((bf16[400,256]{1,0:T(8,128)(2,1)S(1)}, bf16[400,256]{1,0:T(8,128)(2,1)S(1)}, u32[]{:S(2)}, u32[]{:S(2)}) %collective-permute-start.16) | collective-permute-done | bytes 204832 | tf_op jit(solution)/shard_map/ppermute | solution.py:109
  270.2 5.5 %collective-permute-done.17 = bf16[400,256]{1,0:T(8,128)(2,1)S(1)} collective-permute-done((bf16[400,256]{1,0:T(8,128)(2,1)S(1)}, bf16[400,256]{1,0:T(8,128)(2,1)S(1)}, u32[]{:S(2)}, u32[]{:S(2)}) %collective-permute-start.17) | collective-permute-done | bytes 204832 | tf_op jit(solution)/shard_map/ppermute | solution.py:109
  275.7 0.8 multiply_convert_fusion
  276.8 0.7 broadcast_in_dim.66.gates_ref
  277.4 5.9 %collective-permute-done.18.refs_3_ = bf16[16,224,512]{2,1,0:T(8,128)(2,1)} collective-permute-done((bf16[16,224,512]{2,1,0:T(8,128)(2,1)}, bf16[16,224,512]{2,1,0:T(8,128)(2,1)}, u32[]{:S(2)}, u32[]{:S(2)}) %collective-permute-start.18) | collective-permute-done | bytes 3670048 | tf_op jit(solution)/shard_map/ppermute | solution.py:157
  283.3 24.6 %all-gather.3.cloned.1.call-done.refs_0_ = bf16[6400,256]{1,0:T(8,128)(2,1)} async-done(((bf16[400,256]{1,0:T(8,128)(2,1)}), bf16[6400,256]{1,0:T(8,128)(2,1)}) %all-gather.3.cloned.1.call-update) | async-done | bytes 3276816 | tf_op jit(solution)/shard_map/all_gather | solution.py:130
  307.9 70.6 %all-gather.5.cloned.1.call-done.refs_1_ = bf16[6400,256]{1,0:T(8,128)(2,1)} async-done(((bf16[400,256]{1,0:T(8,128)(2,1)}), bf16[6400,256]{1,0:T(8,128)(2,1)}) %all-gather.5.cloned.1.call-update) | async-done | bytes 3276816 | tf_op jit(solution)/shard_map/all_gather | solution.py:130
  378.5 48.2 %shard_map.66 = f32[2,768,224]{2,1,0:T(8,128)} custom-call(s32[16]{0:T(128)} %copy-done.8, s32[16]{0:T(128)} %get-tuple-element.64.chunks, s32[16]{0:T(128)} %get-tuple-element.68.order, s32[1]{0:T(128)} %bitcast.3.mine, s32[16,1,768]{2,1,0:T(1,128)} %broadcast_in_dim.63.refs_0_.slots_ref, f32[16,1,768]{2,1,0:T(1,128)} %broadcast_in_dim.66.gates_ref, ...), custom_call_target="tpu_custom_call" | custom-call | flops 11744051200 | bytes 20000000 | tf_op jit(solution)/shard_map/pallas_call | solution.py:218
  426.7 1.3 slice_bitcast_fusion
  428.4 2.3 collective-permute-done.19
  430.6 1.4 copy.92
  432.2 16.8 %all_to_all.10 = bf16[3,16,16,224]{3,2,0,1:T(8,128)(2,1)S(1)} all-to-all(bf16[3,16,16,224]{3,2,0,1:T(8,128)(2,1)S(1)} %copy.93), channel_id=1, replica_groups=mesh['fsdp'=2,'expert'=16] {'expert'}, dimensions={1} | all-to-all | bytes 688128 | tf_op jit(solution)/shard_map/all_to_all | solution.py:235
  449.1 1.3 reshape.143
  (79 shorter events, 7.4 us)
Async XLA Ops:
  6.5 9.2 %copy-start.5 = (s32[3,16,8]{1,2,0:T(8,128)S(1)}, s32[3,16,8]{1,2,0:T(8,128)}, u32[]{:S(2)}) copy-start(s32[3,16,8]{1,2,0:T(8,128)} %param.7) | copy-start | bytes 4612
  6.5 9.2 %copy-start.6 = (bf16[3,16,8]{1,2,0:T(8,128)(2,1)S(1)}, bf16[3,16,8]{1,2,0:T(8,128)(2,1)}, u32[]{:S(2)}) copy-start(bf16[3,16,8]{1,2,0:T(8,128)(2,1)} %param.8) | copy-start | bytes 2308
  6.5 9.3 %copy-start.4 = (bf16[3,16,7168]{2,1,0:T(8,128)(2,1)S(1)}, bf16[3,16,7168]{2,1,0:T(8,128)(2,1)}, u32[]{:S(2)}) copy-start(bf16[3,16,7168]{2,1,0:T(8,128)(2,1)} %param.6) | copy-start | bytes 2064388
  15.2 37.2 %collective-permute-start = (bf16[16,224,512]{2,1,0:T(8,128)(2,1)}, bf16[16,224,512]{2,1,0:T(8,128)(2,1)}, u32[]{:S(2)}, u32[]{:S(2)}) collective-permute-start(bf16[16,224,512]{2,1,0:T(8,128)(2,1)} %get-tuple-element.51), channel_id=1, source_target_pairs={{0,16},{16,0},{1,17},{17,1},{2,18},{18,2},{3,19},{19,3},{4,20},{20... | collective-permute-start | bytes 11010056 | tf_op jit(solution)/shard_map/ppermute | solution.py:157
  15.7 36.8 %collective-permute-start.1 = (bf16[16,224,512]{2,1,0:T(8,128)(2,1)}, bf16[16,224,512]{2,1,0:T(8,128)(2,1)}, u32[]{:S(2)}, u32[]{:S(2)}) collective-permute-start(bf16[16,224,512]{2,1,0:T(8,128)(2,1)} %get-tuple-element.50), channel_id=1, source_target_pairs={{0,16},{16,0},{1,17},{17,1},{2,18},{18,2},{3,19},{19,3},{4,20},{20... | collective-permute-start | bytes 11010056 | tf_op jit(solution)/shard_map/ppermute | solution.py:157
  19.4 28.8 %copy-start.9 = (s32[16]{0:T(128)S(1)}, s32[16]{0:T(128)}, u32[]{:S(2)}) copy-start(s32[16]{0:T(128)} %param.9) | copy-start | bytes 196
  19.4 28.4 %all-to-all-start = ((bf16[16,3,16,464]{3,2,1,0:T(8,128)(2,1)}), bf16[16,3,16,464]{3,2,1,0:T(8,128)(2,1)S(1)}, u32[]{:S(2)}, u32[]{:S(2)}) async-start(bf16[16,3,16,464]{3,2,1,0:T(8,128)(2,1)} %pad_maximum_fusion), calls=%async_computation | async-start | bytes 1572864 | tf_op jit(solution)/shard_map/all_to_all | solution.py:164
  27.9 21.5 %copy-start.7 = (s32[16]{0:T(128)S(1)}, s32[16]{0:T(128)}, u32[]{:S(2)}) copy-start(s32[16]{0:T(128)} %param.10) | copy-start | bytes 196
  27.9 280.1 %all-gather.3.cloned.1.call-start = ((), (), s32[]{:S(2)}) async-start(), calls=%async_computation.2 | async-start | bytes 3481600 | tf_op jit(solution)/shard_map/all_gather | solution.py:130
  50.0 2.4 copy-start.8
  86.0 35.0 %collective-permute-start.2 = (bf16[2,2,2,400,256]{4,3,1,0,2:T(8,128)(2,1)}, bf16[2,2,2,400,256]{4,3,1,0,2:T(8,128)(2,1)}, u32[]{:S(2)}, u32[]{:S(2)}) collective-permute-start(bf16[2,2,2,400,256]{4,3,1,0,2:T(8,128)(2,1)} %bitcast.103), channel_id=1, source_target_pairs={{0,1},{1,0},{2,3},{3,2},{4,5},{5,4},{6,7},{7,6},{8,9},{9,8},{10,11... | collective-permute-start | bytes 4915208 | tf_op jit(solution)/shard_map/ppermute | solution.py:109
  89.4 35.4 %collective-permute-start.3 = (bf16[2,2,2,400,256]{4,3,1,0,2:T(8,128)(2,1)}, bf16[2,2,2,400,256]{4,3,1,0,2:T(8,128)(2,1)}, u32[]{:S(2)}, u32[]{:S(2)}) collective-permute-start(bf16[2,2,2,400,256]{4,3,1,0,2:T(8,128)(2,1)} %bitcast.102), channel_id=1, source_target_pairs={{0,2},{1,3},{2,0},{3,1},{4,6},{5,7},{6,4},{7,5},{8,10},{9,11},{10,... | collective-permute-start | bytes 4915208 | tf_op jit(solution)/shard_map/ppermute | solution.py:109
  115.5 30.8 %copy-start = (bf16[1,6400,256]{2,1,0:T(8,128)(2,1)}, bf16[1,6400,256]{2,1,0:T(8,128)(2,1)S(1)}, u32[]{:S(2)}) copy-start(bf16[1,6400,256]{2,1,0:T(8,128)(2,1)S(1)} %get-tuple-element.53) | copy-start | bytes 9830404
  121.0 3.7 copy-start.2
  126.6 16.8 %collective-permute-start.4 = (bf16[2,2,400,256]{3,2,1,0:T(8,128)(2,1)S(1)}, bf16[2,2,400,256]{3,2,1,0:T(8,128)(2,1)S(1)}, u32[]{:S(2)}, u32[]{:S(2)}) collective-permute-start(bf16[2,2,400,256]{3,2,1,0:T(8,128)(2,1)S(1)} %fusion.18), channel_id=1, source_target_pairs={{0,2},{1,3},{2,0},{3,1},{4,6},{5,7},{6,4},{7,5},{8,10},{9,11},{10,... | collective-permute-start | bytes 2457608 | tf_op jit(solution)/shard_map/ppermute | solution.py:109
  128.5 16.5 %collective-permute-start.5 = (bf16[2,2,400,256]{3,2,1,0:T(8,128)(2,1)S(1)}, bf16[2,2,400,256]{3,2,1,0:T(8,128)(2,1)S(1)}, u32[]{:S(2)}, u32[]{:S(2)}) collective-permute-start(bf16[2,2,400,256]{3,2,1,0:T(8,128)(2,1)S(1)} %fusion.19), channel_id=1, source_target_pairs={{0,1},{1,0},{2,3},{3,2},{4,5},{5,4},{6,7},{7,6},{8,9},{9,8},{10,11... | collective-permute-start | bytes 2457608 | tf_op jit(solution)/shard_map/ppermute | solution.py:109
  147.7 43.8 %collective-permute-start.8 = (bf16[2,2,2,400,256]{4,3,1,0,2:T(8,128)(2,1)}, bf16[2,2,2,400,256]{4,3,1,0,2:T(8,128)(2,1)}, u32[]{:S(2)}, u32[]{:S(2)}) collective-permute-start(bf16[2,2,2,400,256]{4,3,1,0,2:T(8,128)(2,1)} %copy_bitcast_fusion.3), channel_id=1, source_target_pairs={{0,1},{1,0},{2,3},{3,2},{4,5},{5,4},{6,7},{7,6},{8,9},{9,8},{10,11... | collective-permute-start | bytes 4915208 | tf_op jit(solution)/shard_map/ppermute | solution.py:109
  150.4 42.9 %collective-permute-start.9 = (bf16[2,2,2,400,256]{4,3,1,0,2:T(8,128)(2,1)}, bf16[2,2,2,400,256]{4,3,1,0,2:T(8,128)(2,1)}, u32[]{:S(2)}, u32[]{:S(2)}) collective-permute-start(bf16[2,2,2,400,256]{4,3,1,0,2:T(8,128)(2,1)} %copy_bitcast_fusion.2), channel_id=1, source_target_pairs={{0,2},{1,3},{2,0},{3,1},{4,6},{5,7},{6,4},{7,5},{8,10},{9,11},{10,... | collective-permute-start | bytes 4915208 | tf_op jit(solution)/shard_map/ppermute | solution.py:109
  153.9 29.5 %collective-permute-start.6 = (bf16[2,400,256]{2,1,0:T(8,128)(2,1)}, bf16[2,400,256]{2,1,0:T(8,128)(2,1)}, u32[]{:S(2)}, u32[]{:S(2)}) collective-permute-start(bf16[2,400,256]{2,1,0:T(8,128)(2,1)} %fusion.24), channel_id=1, source_target_pairs={{0,8},{1,9},{2,10},{3,11},{4,12},{5,13},{6,14},{7,15},{8,0},{9,1},... | collective-permute-start | bytes 1228808 | tf_op jit(solution)/shard_map/ppermute | solution.py:109
  159.3 30.9 %collective-permute-start.7 = (bf16[2,400,256]{2,1,0:T(8,128)(2,1)}, bf16[2,400,256]{2,1,0:T(8,128)(2,1)}, u32[]{:S(2)}, u32[]{:S(2)}) collective-permute-start(bf16[2,400,256]{2,1,0:T(8,128)(2,1)} %fusion.25), channel_id=1, source_target_pairs={{0,8},{1,9},{2,10},{3,11},{4,12},{5,13},{6,14},{7,15},{8,0},{9,1},... | collective-permute-start | bytes 1228808 | tf_op jit(solution)/shard_map/ppermute | solution.py:109
  159.3 32.2 %copy-start.1 = (bf16[1,6400,256]{2,1,0:T(8,128)(2,1)S(1)}, bf16[1,6400,256]{2,1,0:T(8,128)(2,1)}, u32[]{:S(2)}) copy-start(bf16[1,6400,256]{2,1,0:T(8,128)(2,1)} %copy-done) | copy-start | bytes 9830404
  195.2 19.2 %collective-permute-start.12 = (bf16[2,2,400,256]{3,2,1,0:T(8,128)(2,1)S(1)}, bf16[2,2,400,256]{3,2,1,0:T(8,128)(2,1)S(1)}, u32[]{:S(2)}, u32[]{:S(2)}) collective-permute-start(bf16[2,2,400,256]{3,2,1,0:T(8,128)(2,1)S(1)} %fusion.20), channel_id=1, source_target_pairs={{0,2},{1,3},{2,0},{3,1},{4,6},{5,7},{6,4},{7,5},{8,10},{9,11},{10,... | collective-permute-start | bytes 2457608 | tf_op jit(solution)/shard_map/ppermute | solution.py:109
  196.8 8.1 %collective-permute-start.10 = (bf16[400,256]{1,0:T(8,128)(2,1)S(1)}, bf16[400,256]{1,0:T(8,128)(2,1)S(1)}, u32[]{:S(2)}, u32[]{:S(2)}) collective-permute-start(bf16[400,256]{1,0:T(8,128)(2,1)S(1)} %fusion.29), channel_id=1, source_target_pairs={{0,4},{1,5},{2,6},{3,7},{4,0},{5,1},{6,2},{7,3},{8,12},{9,13},{10,... | collective-permute-start | bytes 614408 | tf_op jit(solution)/shard_map/ppermute | solution.py:109
  197.0 19.5 %collective-permute-start.13 = (bf16[2,2,400,256]{3,2,1,0:T(8,128)(2,1)S(1)}, bf16[2,2,400,256]{3,2,1,0:T(8,128)(2,1)S(1)}, u32[]{:S(2)}, u32[]{:S(2)}) collective-permute-start(bf16[2,2,400,256]{3,2,1,0:T(8,128)(2,1)S(1)} %fusion.21), channel_id=1, source_target_pairs={{0,1},{1,0},{2,3},{3,2},{4,5},{5,4},{6,7},{7,6},{8,9},{9,8},{10,11... | collective-permute-start | bytes 2457608 | tf_op jit(solution)/shard_map/ppermute | solution.py:109
  198.3 8.8 %collective-permute-start.11 = (bf16[400,256]{1,0:T(8,128)(2,1)S(1)}, bf16[400,256]{1,0:T(8,128)(2,1)S(1)}, u32[]{:S(2)}, u32[]{:S(2)}) collective-permute-start(bf16[400,256]{1,0:T(8,128)(2,1)S(1)} %fusion.30), channel_id=1, source_target_pairs={{0,4},{1,5},{2,6},{3,7},{4,0},{5,1},{6,2},{7,3},{8,12},{9,13},{10,... | collective-permute-start | bytes 614408 | tf_op jit(solution)/shard_map/ppermute | solution.py:109
  217.5 161.1 %all-gather.5.cloned.1.call-start = ((), (), s32[]{:S(2)}) async-start(), calls=%async_computation.3 | async-start | bytes 3481600 | tf_op jit(solution)/shard_map/all_gather | solution.py:130
  217.6 33.7 %collective-permute-start.14 = (bf16[2,400,256]{2,1,0:T(8,128)(2,1)S(1)}, bf16[2,400,256]{2,1,0:T(8,128)(2,1)S(1)}, u32[]{:S(2)}, u32[]{:S(2)}) collective-permute-start(bf16[2,400,256]{2,1,0:T(8,128)(2,1)S(1)} %fusion.26), channel_id=1, source_target_pairs={{0,8},{1,9},{2,10},{3,11},{4,12},{5,13},{6,14},{7,15},{8,0},{9,1},... | collective-permute-start | bytes 1228808 | tf_op jit(solution)/shard_map/ppermute | solution.py:109
  219.4 39.6 %collective-permute-start.15 = (bf16[2,400,256]{2,1,0:T(8,128)(2,1)S(1)}, bf16[2,400,256]{2,1,0:T(8,128)(2,1)S(1)}, u32[]{:S(2)}, u32[]{:S(2)}) collective-permute-start(bf16[2,400,256]{2,1,0:T(8,128)(2,1)S(1)} %fusion.27), channel_id=1, source_target_pairs={{0,8},{1,9},{2,10},{3,11},{4,12},{5,13},{6,14},{7,15},{8,0},{9,1},... | collective-permute-start | bytes 1228808 | tf_op jit(solution)/shard_map/ppermute | solution.py:109
  259.1 11.0 %collective-permute-start.16 = (bf16[400,256]{1,0:T(8,128)(2,1)S(1)}, bf16[400,256]{1,0:T(8,128)(2,1)S(1)}, u32[]{:S(2)}, u32[]{:S(2)}) collective-permute-start(bf16[400,256]{1,0:T(8,128)(2,1)S(1)} %fusion.31), channel_id=1, source_target_pairs={{0,4},{1,5},{2,6},{3,7},{4,0},{5,1},{6,2},{7,3},{8,12},{9,13},{10,... | collective-permute-start | bytes 614408 | tf_op jit(solution)/shard_map/ppermute | solution.py:109
  259.3 16.4 %collective-permute-start.17 = (bf16[400,256]{1,0:T(8,128)(2,1)S(1)}, bf16[400,256]{1,0:T(8,128)(2,1)S(1)}, u32[]{:S(2)}, u32[]{:S(2)}) collective-permute-start(bf16[400,256]{1,0:T(8,128)(2,1)S(1)} %fusion.32), channel_id=1, source_target_pairs={{0,4},{1,5},{2,6},{3,7},{4,0},{5,1},{6,2},{7,3},{8,12},{9,13},{10,... | collective-permute-start | bytes 614408 | tf_op jit(solution)/shard_map/ppermute | solution.py:109
  276.5 6.8 %collective-permute-start.18 = (bf16[16,224,512]{2,1,0:T(8,128)(2,1)}, bf16[16,224,512]{2,1,0:T(8,128)(2,1)}, u32[]{:S(2)}, u32[]{:S(2)}) collective-permute-start(bf16[16,224,512]{2,1,0:T(8,128)(2,1)} %get-tuple-element.49), channel_id=1, source_target_pairs={{0,16},{16,0},{1,17},{17,1},{2,18},{18,2},{3,19},{19,3},{4,20},{20... | collective-permute-start | bytes 11010056 | tf_op jit(solution)/shard_map/ppermute | solution.py:157
  426.7 5.3 %copy-start.3 = (f32[2,768,224]{2,1,0:T(8,128)S(1)}, f32[2,768,224]{2,1,0:T(8,128)}, u32[]{:S(2)}) copy-start(f32[2,768,224]{2,1,0:T(8,128)} %shard_map.66) | copy-start | bytes 4128772
  428.3 2.3 collective-permute-start.19
Sparse Core Ops, SparseCore 0:
  217.6 90.3 all-gather.2
  310.7 67.7 all-gather.4

commit v3 on v2

--- a/solution.py
+++ b/solution.py
@@ -7,7 +7,7 @@
 from jax.experimental.pallas import tpu as pltpu
 from jax.sharding import PartitionSpec as P
 
-TILE = 128
+TILE = 256
 HALVES = 2
 ALIGN = 16
 BF16 = jnp.bfloat16
@@ -74,9 +74,9 @@
 
 
 def down_kernel(parts, starts, chunks, order, mine, slots_ref, gates_ref, *refs):
-    h_refs, weights, out_ref = refs[:HALVES], refs[HALVES:-1], refs[-1]
+    h_refs, weights, out_ref = refs[: 2 * HALVES], refs[2 * HALVES : -1], refs[-1]
     e = pl.program_id(0)
-    total, cols = h_refs[0].shape
+    total = h_refs[0].shape[0]
 
     @pl.when(e == 0)
     def _():
@@ -90,12 +90,13 @@
         base = pl.multiple_of(jnp.minimum(first, total - TILE), ALIGN)
         number = base + lax.broadcasted_iota(jnp.int32, (TILE, slots.shape[1]), 0)
         mix = jnp.where((slots == number) & (number >= first), gates, 0.0).astype(BF16)
-        h = [h_ref[pl.ds(base, TILE), :] for h_ref in h_refs]
+        h = jnp.concatenate([h_ref[pl.ds(base, TILE), :] for h_ref in h_refs], axis=1)
+        mix = jnp.concatenate([mix, mix], axis=0)
         for i in range(parts):
-            y = sum(dot(h[q], weights[i][0, :, q * cols : (q + 1) * cols], 1, 1) for q in range(HALVES))
+            y = dot(h, weights[i][0], 1, 1)
             high = y.astype(BF16)
             low = (y - high.astype(F32)).astype(BF16)
-            out_ref[i] += dot(mix, high, 0, 0) + dot(mix, low, 0, 0)
+            out_ref[i] += dot(mix, jnp.concatenate([high, low], axis=0), 0, 0)
         return carry
 
     lax.fori_loop(0, chunks[e], step, 0)
@@ -110,25 +111,35 @@
     return keep + got.astype(F32), [i for i in left if i != b]
 
 
-def reduce_all(pieces, n):
+def double(cur, have, b, n):
+    axis = sum(i > b for i in have)
+    first = ((lax.axis_index("expert") >> b) & 1) == 0
+    got = lax.ppermute(cur, "expert", [(i, i ^ (1 << b)) for i in range(n)])
+    low, high = jnp.where(first, cur, got), jnp.where(first, got, cur)
+    return jnp.stack([low, high], axis), sorted(have + [b], reverse=True)
+
+
+def exchange_all(pieces, n):
     bits = n.bit_length() - 1
-    later = list(range(bits - 1, 1, -1))
+    later = list(range(2, bits))
     orders = ([0, 1] + later, [1, 0] + later)
     left = list(range(bits - 1, -1, -1))
     state = [[(i.reshape((2,) * bits + (i.shape[0] // n, i.shape[1])), left) for i in pair] for pair in pieces]
-    done = [None] * len(state)
-    for turn in range(bits + 2 * (len(state) - 1)):
+    for turn in range(2 * bits + 2 * (len(state) - 1)):
         for q in range(len(state)):
             at = turn - 2 * q
             if 0 <= at < bits:
                 state[q] = [halve(*state[q][k], orders[k][at], n) for k in range(2)]
+            if at == bits - 1:
+                a, b = (i for i, _ in state[q])
+                h = (a * jax.nn.sigmoid(a) * b).astype(BF16)
+                cols = h.shape[1] // 2
+                state[q] = [(h[:, :cols], []), (h[:, cols:], [])]
+            if bits <= at < 2 * bits:
+                state[q] = [double(*state[q][k], orders[k][2 * bits - 1 - at], n) for k in range(2)]
         held = lax.optimization_barrier([[i for i, _ in pair] for pair in state])
         state = [[(i, pair[k][1]) for k, i in enumerate(new)] for new, pair in zip(held, state)]
-        for q in range(len(state)):
-            if turn - 2 * q == bits - 1:
-                a, b = (i for i, _ in state[q])
-                done[q] = lax.all_gather((a * jax.nn.sigmoid(a) * b).astype(BF16), "expert", axis=0, tiled=True)
-    return done
+    return [i.reshape(-1, i.shape[-1]) for pair in state for i, _ in pair]
 
 
 def body(tokens, route_ids, gate_values, cap_limit, update_ids, expert_weights):
@@ -209,7 +220,7 @@
             xs = made[1]
         ab = made[0]
         pieces.append([ab[0, :packed], ab[1, :packed]])
-    hs = reduce_all(pieces, owners)
+    hs = exchange_all(pieces, owners)
     down_specs, down_args = [own(2, share, 0)], [expert_weights]
     for got in others:
         down_specs.append(other(share, 0))
@@ -221,7 +232,7 @@
         grid_spec=pltpu.PrefetchScalarGridSpec(
             num_scalar_prefetch=4,
             grid=(experts,),
-            in_specs=[line, line, *[whole(packed, cols)] * HALVES] + down_specs,
+            in_specs=[line, line, *[whole(packed, cols // 2)] * (2 * HALVES)] + down_specs,
             out_specs=whole(parts, rows, local),
         ),
         compiler_params=params,

time: 460 us -> 391 us (0.85)
  waiting for transfers between devices: 242 us -> 163 us
  starting transfers between devices: 31.5 us -> 53.3 us
  Pallas kernels: 98.1 us -> 78.3 us
  between operations: 13.9 us -> 0.71 us
  other arithmetic: 18.7 us -> 29.1 us
  local copies, waits for them, and re-layouts: 35.7 us -> 43.3 us
    all_gather x2 -> x0, waiting for transfers between devices: 95.2 us -> none  [reduce_all(): lax.all_gather((a * jax.nn.sigmoid(a) * b).astype(BF16), 'expert', axis=0...]
    ppermute x0 -> x16, waiting for transfers between devices: none -> 57.2 us  [double(): got = lax.ppermute(cur, 'expert', [(i, i ^ 1 << b) for i in range(n)])]
    ppermute x16, waiting for transfers between devices: 119 us -> 83.4 us  [halve(): got = lax.ppermute(send, 'expert', [(i, i ^ 1 << b) for i in range(n)])]
    ppermute x0 -> x16, starting transfers between devices: none -> 18.9 us  [double(): got = lax.ppermute(cur, 'expert', [(i, i ^ 1 << b) for i in range(n)])]
    pallas_call x1, Pallas kernels: 48.2 us -> 33.1 us  [body(): pl.pallas_call(functools.partial(down_kernel, parts), out_shape=jax.Shape...]
    another operation x0 -> x32, other arithmetic: none -> 7.81 us  [double(): return (jnp.stack([low, high], axis), sorted(have + [b], reverse=True))]
    ppermute x3, waiting for transfers between devices: 5.91 us -> 0.01 us  [body(): others.append([lax.ppermute(cut, 'fsdp', pairs) for cut in cuts])]
    pallas_call x2, Pallas kernels: 49.9 us -> 45.1 us  [body(): pl.pallas_call(functools.partial(up_kernel, parts, fresh), out_shape=[jax...]
  transfers between devices with their start and end apart: 23 -> 37, of which waited for: 19 -> 30; matrix products, arithmetic and copies ran while one was open for 7% -> 12% of each run, Pallas kernels for 5% -> 5%
where the time goes in v3:
time: 391 us; the launch traced here: 389 us
  waiting for transfers between devices  163 us (42%)
  Pallas kernels  78.3 us (20%)
  starting transfers between devices  53.3 us (14%)
  local copies, waits for them, and re-layouts  43.3 us (11%)
  other arithmetic  29.1 us (7%)
  blocking collectives  20.2 us (5%)
    ppermute x16, waiting for transfers between devices, halve(): got = lax.ppermute(send, 'expert', [(i, i ^ 1 << b) for i in range(n)])  83.4 us
    ppermute x16, waiting for transfers between devices, double(): got = lax.ppermute(cur, 'expert', [(i, i ^ 1 << b) for i in range(n)])  57.2 us
    pallas_call x2, Pallas kernels, body(): pl.pallas_call(functools.partial(up_kernel, parts, fresh), out_shape=[jax...  45.1 us
    pallas_call x1, Pallas kernels, body(): pl.pallas_call(functools.partial(down_kernel, parts), out_shape=jax.Shape...  33.1 us
    ppermute x16, starting transfers between devices, halve(): got = lax.ppermute(send, 'expert', [(i, i ^ 1 << b) for i in range(n)])  25.5 us
    all_to_all x1, blocking collectives, body(): y = lax.all_to_all(y, 'expert', split_axis=1, concat_axis=1, tiled=True)  20.2 us
    all_to_all x1, waiting for transfers between devices, body(): x = lax.all_to_all(x, 'expert', split_axis=0, concat_axis=0, tiled=True)  19.8 us
    ppermute x16, starting transfers between devices, double(): got = lax.ppermute(cur, 'expert', [(i, i ^ 1 << b) for i in range(n)])  18.9 us
  transfers between devices with their start and end apart: 37, of which 30 were waited for; matrix products, arithmetic and copies ran while one was open for 12% of the time, Pallas kernels for 5%

profile of v3, /device:TPU:0, one launch (start us, length us, event | category | flops | bytes accessed | tf_op | source)
XLA Modules:
  0.0 388.6 jit_solution(8800210318117707295)
XLA Ops:
  0.0 8.7 %constant_dynamic-slice_fusion = (bf16[16,224,512]{2,1,0:T(8,128)(2,1)}, bf16[16,224,512]{2,1,0:T(8,128)(2,1)}, bf16[16,224,512]{2,1,0:T(8,128)(2,1)}) fusion(bf16[16,224,3072]{2,1,0:T(8,128)(2,1)} %refs_4_.1, s32[]{:T(128)S(6)} %select_n.339, s32[]{:T(128)S(6)} %select_n.296, s32[]{:T(128)S(6)} %select_n.295), kind=kLoop, calls=%fused_computation.124 | loop fusion | bytes 22020108 | tf_op jit(solution)/shard_map/dynamic_slice | solution.py:165
  12.9 8.3 %all-to-all-start = ((bf16[16,3,16,464]{3,2,1,0:T(8,128)(2,1)}), bf16[16,3,16,464]{3,2,1,0:T(8,128)(2,1)S(1)}, u32[]{:S(2)}, u32[]{:S(2)}) async-start(bf16[16,3,16,464]{3,2,1,0:T(8,128)(2,1)} %pad_maximum_fusion.8), calls=%async_computation | async-start | bytes 1572864 | tf_op jit(solution)/shard_map/all_to_all | solution.py:175
  21.3 19.8 %all-to-all-done = bf16[16,3,16,464]{3,2,1,0:T(8,128)(2,1)S(1)} async-done(((bf16[16,3,16,464]{3,2,1,0:T(8,128)(2,1)}), bf16[16,3,16,464]{3,2,1,0:T(8,128)(2,1)S(1)}, u32[]{:S(2)}, u32[]{:S(2)}) %all-to-all-start) | async-done | bytes 712736 | tf_op jit(solution)/shard_map/all_to_all | solution.py:175
  45.8 25.6 %shard_map.64 = (bf16[2,6656,256]{2,1,0:T(8,128)(2,1)}, bf16[2,6656,224]{2,1,0:T(8,128)(2,1)}) custom-call(s32[16]{0:T(128)} %copy-done.14, s32[16]{0:T(128)} %get-tuple-element.140.chunks, s32[16]{0:T(128)} %get-tuple-element.144.order, s32[1]{0:T(128)} %bitcast.3.mine, s32[16,1,768]{2,1,0:T(1,128)} %broadcast_in_dim.63.refs_0_.slots_ref, ...), custom_call_target="tpu_custom_call" | custom-call | flops 20000000000 | bytes 50000000 | tf_op jit(solution)/shard_map/pallas_call | solution.py:207
  71.4 3.3 fusion.42
  76.9 1.4 constant_dynamic-slice_fusion.4
  79.6 1.6 collective-permute-start.3
  81.2 19.5 %shard_map.65 = bf16[2,6656,256]{2,1,0:T(8,128)(2,1)} custom-call(s32[16]{0:T(128)} %copy-done.14, s32[16]{0:T(128)} %get-tuple-element.140.chunks, s32[16]{0:T(128)} %get-tuple-element.144.order, s32[1]{0:T(128)} %bitcast.3.mine, bf16[2,6656,224]{2,1,0:T(8,128)(2,1)} %get-tuple-element.48.refs_0_, bf16[16,224,3072]{2,1,0:T(8,128)(2,1)} %refs_4_.1, ...), custom_call_target="tpu_custom_call" | custom-call | flops 20000000000 | bytes 50000000 | tf_op jit(solution)/shard_map/pallas_call | solution.py:207
  100.8 3.3 fusion.41
  104.1 7.2 %collective-permute-done.2 = bf16[2,2,2,400,256]{4,3,0,1,2:T(8,128)(2,1)} collective-permute-done((bf16[2,2,2,400,256]{4,3,0,1,2:T(8,128)(2,1)}, bf16[2,2,2,400,256]{4,3,0,1,2:T(8,128)(2,1)}, u32[]{:S(2)}, u32[]{:S(2)}) %collective-permute-start.2) | collective-permute-done | bytes 1638432 | tf_op jit(solution)/shard_map/ppermute | solution.py:110
  111.3 1.9 convert_add_fusion.3
  113.2 1.7 collective-permute-done.3
  115.0 1.8 convert_add_fusion.2
  116.9 1.8 collective-permute-start.4
  118.8 1.5 collective-permute-start.5
  120.3 13.3 %collective-permute-done.4 = bf16[2,2,400,256]{3,2,0,1:T(8,128)(2,1)S(1)} collective-permute-done((bf16[2,2,400,256]{3,2,0,1:T(8,128)(2,1)S(1)}, bf16[2,2,400,256]{3,2,0,1:T(8,128)(2,1)S(1)}, u32[]{:S(2)}, u32[]{:S(2)}) %collective-permute-start.4) | collective-permute-done | bytes 819232 | tf_op jit(solution)/shard_map/ppermute | solution.py:110
  133.6 1.4 bitcast_add_fusion.3
  137.9 1.5 collective-permute-start.8
  140.7 1.5 collective-permute-start.9
  142.2 1.9 fusion.24
  144.1 3.7 collective-permute-start.6
  147.8 1.9 fusion.25
  149.8 8.5 %collective-permute-done.6 = bf16[2,400,256]{2,1,0:T(8,128)(2,1)} collective-permute-done((bf16[2,400,256]{2,1,0:T(8,128)(2,1)}, bf16[2,400,256]{2,1,0:T(8,128)(2,1)}, u32[]{:S(2)}, u32[]{:S(2)}) %collective-permute-start.6) | collective-permute-done | bytes 409632 | tf_op jit(solution)/shard_map/ppermute | solution.py:110
  159.6 3.0 collective-permute-done.7
  164.0 7.3 %collective-permute-done.8 = bf16[2,2,2,400,256]{4,3,0,1,2:T(8,128)(2,1)} collective-permute-done((bf16[2,2,2,400,256]{4,3,0,1,2:T(8,128)(2,1)}, bf16[2,2,2,400,256]{4,3,0,1,2:T(8,128)(2,1)}, u32[]{:S(2)}, u32[]{:S(2)}) %collective-permute-start.8) | collective-permute-done | bytes 1638432 | tf_op jit(solution)/shard_map/ppermute | solution.py:110
  171.3 1.8 convert_add_fusion.1
  173.8 2.2 convert_add_fusion
  177.1 1.8 collective-permute-start.12
  179.6 6.2 %collective-permute-start.11 = (bf16[400,256]{1,0:T(8,128)(2,1)}, bf16[400,256]{1,0:T(8,128)(2,1)}, u32[]{:S(2)}, u32[]{:S(2)}) collective-permute-start(bf16[400,256]{1,0:T(8,128)(2,1)} %fusion.34), channel_id=1, source_target_pairs={{0,8},{1,9},{2,10},{3,11},{4,12},{5,13},{6,14},{7,15},{8,0},{9,1},... | collective-permute-start | bytes 614408 | tf_op jit(solution)/shard_map/ppermute | solution.py:110
  187.7 8.7 %collective-permute-done.11 = bf16[400,256]{1,0:T(8,128)(2,1)} collective-permute-done((bf16[400,256]{1,0:T(8,128)(2,1)}, bf16[400,256]{1,0:T(8,128)(2,1)}, u32[]{:S(2)}, u32[]{:S(2)}) %collective-permute-start.11) | collective-permute-done | bytes 204832 | tf_op jit(solution)/shard_map/ppermute | solution.py:110
  196.4 4.2 %collective-permute-done.10 = bf16[400,256]{1,0:T(8,128)(2,1)} collective-permute-done((bf16[400,256]{1,0:T(8,128)(2,1)}, bf16[400,256]{1,0:T(8,128)(2,1)}, u32[]{:S(2)}, u32[]{:S(2)}) %collective-permute-start.10) | collective-permute-done | bytes 204832 | tf_op jit(solution)/shard_map/ppermute | solution.py:110
  200.6 1.4 fusion.31
  202.1 1.5 bitcast_add_fusion.1
  205.6 2.3 collective-permute-start.14
  208.9 2.0 collective-permute-start.17
  210.8 3.4 collective-permute-done.14
  214.2 1.5 collective-permute-done.15
  215.8 8.1 %collective-permute-done.16 = bf16[2,400,256]{2,1,0:T(8,128)(2,1)S(1)} collective-permute-done((bf16[2,400,256]{2,1,0:T(8,128)(2,1)S(1)}, bf16[2,400,256]{2,1,0:T(8,128)(2,1)S(1)}, u32[]{:S(2)}, u32[]{:S(2)}) %collective-permute-start.16) | collective-permute-done | bytes 409632 | tf_op jit(solution)/shard_map/ppermute | solution.py:110
  224.0 7.9 %collective-permute-done.17 = bf16[2,400,256]{2,1,0:T(8,128)(2,1)S(1)} collective-permute-done((bf16[2,400,256]{2,1,0:T(8,128)(2,1)S(1)}, bf16[2,400,256]{2,1,0:T(8,128)(2,1)S(1)}, u32[]{:S(2)}, u32[]{:S(2)}) %collective-permute-start.17) | collective-permute-done | bytes 409632 | tf_op jit(solution)/shard_map/ppermute | solution.py:110
  232.1 2.0 collective-permute-start.19
  234.2 3.0 collective-permute-start.20
  237.2 5.6 %collective-permute-done.18 = bf16[2,400,128]{2,1,0:T(8,128)(2,1)S(1)} collective-permute-done((bf16[2,400,128]{2,1,0:T(8,128)(2,1)S(1)}, bf16[2,400,128]{2,1,0:T(8,128)(2,1)S(1)}, u32[]{:S(2)}, u32[]{:S(2)}) %collective-permute-start.18) | collective-permute-done | bytes 204832 | tf_op jit(solution)/shard_map/ppermute | solution.py:117
  242.8 9.0 %collective-permute-done.21 = bf16[400,256]{1,0:T(8,128)(2,1)S(1)} collective-permute-done((bf16[400,256]{1,0:T(8,128)(2,1)S(1)}, bf16[400,256]{1,0:T(8,128)(2,1)S(1)}, u32[]{:S(2)}, u32[]{:S(2)}) %collective-permute-start.21) | collective-permute-done | bytes 204832 | tf_op jit(solution)/shard_map/ppermute | solution.py:110
  251.8 3.2 collective-permute-done.20
  255.9 2.8 collective-permute-start.25
  258.7 3.6 collective-permute-done.24
  263.5 2.3 collective-permute-done.22
  266.5 1.7 collective-permute-start.27
  268.1 1.9 collective-permute-start.29
  270.1 2.6 collective-permute-done.28
  272.7 3.6 collective-permute-done.29
  276.4 8.0 %collective-permute-done.26 = bf16[2,2,2,400,128]{4,3,0,1,2:T(8,128)(2,1)S(1)} collective-permute-done((bf16[2,2,2,400,128]{4,3,0,1,2:T(8,128)(2,1)S(1)}, bf16[2,2,2,400,128]{4,3,0,1,2:T(8,128)(2,1)S(1)}, u32[]{:S(2)}, u32[]{:S(2)}) %collective-permute-start.26) | collective-permute-done | bytes 819232 | tf_op jit(solution)/shard_map/ppermute | solution.py:117
  284.7 2.4 collective-permute-done.27
  287.4 1.7 collective-permute-start.30
  289.1 1.7 collective-permute-start.31
  290.9 7.7 %collective-permute-done.30 = bf16[2,2,400,128]{3,2,0,1:T(8,128)(2,1)S(1)} collective-permute-done((bf16[2,2,400,128]{3,2,0,1:T(8,128)(2,1)S(1)}, bf16[2,2,400,128]{3,2,0,1:T(8,128)(2,1)S(1)}, u32[]{:S(2)}, u32[]{:S(2)}) %collective-permute-start.30) | collective-permute-done | bytes 409632 | tf_op jit(solution)/shard_map/ppermute | solution.py:117
  301.0 1.7 collective-permute-start.32
  304.9 15.1 %collective-permute-done.32 = bf16[2,2,2,400,128]{4,3,0,1,2:T(8,128)(2,1)} collective-permute-done((bf16[2,2,2,400,128]{4,3,0,1,2:T(8,128)(2,1)}, bf16[2,2,2,400,128]{4,3,0,1,2:T(8,128)(2,1)}, u32[]{:S(2)}, u32[]{:S(2)}) %collective-permute-start.32) | collective-permute-done | bytes 819232 | tf_op jit(solution)/shard_map/ppermute | solution.py:117
  320.0 1.5 select_bitcast_fusion.3
  321.7 1.5 select_bitcast_fusion.1
  327.1 1.4 copy.168
  328.5 33.1 %shard_map.66 = f32[2,768,224]{2,1,0:T(8,128)} custom-call(s32[16]{0:T(128)} %copy-done.14, s32[16]{0:T(128)} %get-tuple-element.140.chunks, s32[16]{0:T(128)} %get-tuple-element.144.order, s32[1]{0:T(128)} %bitcast.3.mine, s32[16,1,768]{2,1,0:T(1,128)} %broadcast_in_dim.63.refs_0_.slots_ref, f32[16,1,768]{2,1,0:T(1,128)} %broadcast_in_dim.66.gates_ref, ...), custom_call_target="tpu_custom_call" | custom-call | flops 11744051200 | bytes 20000000 | tf_op jit(solution)/shard_map/pallas_call | solution.py:229
  363.1 2.3 collective-permute-done.35
  366.9 20.2 %all_to_all.10 = bf16[3,16,16,224]{3,2,0,1:T(8,128)(2,1)S(1)} all-to-all(bf16[3,16,16,224]{3,2,0,1:T(8,128)(2,1)S(1)} %copy.171), channel_id=1, replica_groups=mesh['fsdp'=2,'expert'=16] {'expert'}, dimensions={1} | all-to-all | bytes 688128 | tf_op jit(solution)/shard_map/all_to_all | solution.py:246
  (150 shorter events, 43.7 us)
Async XLA Ops:
  0.0 9.2 %copy-start.11 = (s32[3,16,8]{1,2,0:T(8,128)S(1)}, s32[3,16,8]{1,2,0:T(8,128)}, u32[]{:S(2)}) copy-start(s32[3,16,8]{1,2,0:T(8,128)} %param.7) | copy-start | bytes 4612
  0.0 9.2 %copy-start.12 = (bf16[3,16,8]{1,2,0:T(8,128)(2,1)S(1)}, bf16[3,16,8]{1,2,0:T(8,128)(2,1)}, u32[]{:S(2)}) copy-start(bf16[3,16,8]{1,2,0:T(8,128)(2,1)} %param.8) | copy-start | bytes 2308
  0.0 9.3 %copy-start.10 = (bf16[3,16,7168]{2,1,0:T(8,128)(2,1)S(1)}, bf16[3,16,7168]{2,1,0:T(8,128)(2,1)}, u32[]{:S(2)}) copy-start(bf16[3,16,7168]{2,1,0:T(8,128)(2,1)} %param.6) | copy-start | bytes 2064388
  8.7 37.1 %collective-permute-start = (bf16[16,224,512]{2,1,0:T(8,128)(2,1)}, bf16[16,224,512]{2,1,0:T(8,128)(2,1)}, u32[]{:S(2)}, u32[]{:S(2)}) collective-permute-start(bf16[16,224,512]{2,1,0:T(8,128)(2,1)} %get-tuple-element.91), channel_id=1, source_target_pairs={{0,16},{16,0},{1,17},{17,1},{2,18},{18,2},{3,19},{19,3},{4,20},{20... | collective-permute-start | bytes 11010056 | tf_op jit(solution)/shard_map/ppermute | solution.py:168
  9.1 36.7 %collective-permute-start.1 = (bf16[16,224,512]{2,1,0:T(8,128)(2,1)}, bf16[16,224,512]{2,1,0:T(8,128)(2,1)}, u32[]{:S(2)}, u32[]{:S(2)}) collective-permute-start(bf16[16,224,512]{2,1,0:T(8,128)(2,1)} %get-tuple-element.90), channel_id=1, source_target_pairs={{0,16},{16,0},{1,17},{17,1},{2,18},{18,2},{3,19},{19,3},{4,20},{20... | collective-permute-start | bytes 11010056 | tf_op jit(solution)/shard_map/ppermute | solution.py:168
  12.9 28.2 %all-to-all-start = ((bf16[16,3,16,464]{3,2,1,0:T(8,128)(2,1)}), bf16[16,3,16,464]{3,2,1,0:T(8,128)(2,1)S(1)}, u32[]{:S(2)}, u32[]{:S(2)}) async-start(bf16[16,3,16,464]{3,2,1,0:T(8,128)(2,1)} %pad_maximum_fusion.8), calls=%async_computation | async-start | bytes 1572864 | tf_op jit(solution)/shard_map/all_to_all | solution.py:175
  21.2 20.3 %copy-start.15 = (s32[16]{0:T(128)S(1)}, s32[16]{0:T(128)}, u32[]{:S(2)}) copy-start(s32[16]{0:T(128)} %param.9) | copy-start | bytes 196
  41.2 1.6 copy-start.13
  43.4 2.4 copy-start.14
  76.4 35.0 %collective-permute-start.2 = (bf16[2,2,2,400,256]{4,3,0,1,2:T(8,128)(2,1)}, bf16[2,2,2,400,256]{4,3,0,1,2:T(8,128)(2,1)}, u32[]{:S(2)}, u32[]{:S(2)}) collective-permute-start(bf16[2,2,2,400,256]{4,3,0,1,2:T(8,128)(2,1)} %bitcast.197), channel_id=1, source_target_pairs={{0,1},{1,0},{2,3},{3,2},{4,5},{5,4},{6,7},{7,6},{8,9},{9,8},{10,11... | collective-permute-start | bytes 4915208 | tf_op jit(solution)/shard_map/ppermute | solution.py:110
  79.6 35.4 %collective-permute-start.3 = (bf16[2,2,2,400,256]{4,3,0,1,2:T(8,128)(2,1)}, bf16[2,2,2,400,256]{4,3,0,1,2:T(8,128)(2,1)}, u32[]{:S(2)}, u32[]{:S(2)}) collective-permute-start(bf16[2,2,2,400,256]{4,3,0,1,2:T(8,128)(2,1)} %bitcast.196), channel_id=1, source_target_pairs={{0,2},{1,3},{2,0},{3,1},{4,6},{5,7},{6,4},{7,5},{8,10},{9,11},{10,... | collective-permute-start | bytes 4915208 | tf_op jit(solution)/shard_map/ppermute | solution.py:110
  104.1 32.5 %copy-start = (bf16[1,6400,256]{2,1,0:T(8,128)(2,1)}, bf16[1,6400,256]{2,1,0:T(8,128)(2,1)S(1)}, u32[]{:S(2)}) copy-start(bf16[1,6400,256]{2,1,0:T(8,128)(2,1)S(1)} %get-tuple-element.93) | copy-start | bytes 9830404
  111.3 3.7 copy-start.6
  116.9 16.8 %collective-permute-start.4 = (bf16[2,2,400,256]{3,2,0,1:T(8,128)(2,1)S(1)}, bf16[2,2,400,256]{3,2,0,1:T(8,128)(2,1)S(1)}, u32[]{:S(2)}, u32[]{:S(2)}) collective-permute-start(bf16[2,2,400,256]{3,2,0,1:T(8,128)(2,1)S(1)} %fusion.18), channel_id=1, source_target_pairs={{0,2},{1,3},{2,0},{3,1},{4,6},{5,7},{6,4},{7,5},{8,10},{9,11},{10,... | collective-permute-start | bytes 2457608 | tf_op jit(solution)/shard_map/ppermute | solution.py:110
  118.8 16.5 %collective-permute-start.5 = (bf16[2,2,400,256]{3,2,0,1:T(8,128)(2,1)S(1)}, bf16[2,2,400,256]{3,2,0,1:T(8,128)(2,1)S(1)}, u32[]{:S(2)}, u32[]{:S(2)}) collective-permute-start(bf16[2,2,400,256]{3,2,0,1:T(8,128)(2,1)S(1)} %fusion.19), channel_id=1, source_target_pairs={{0,1},{1,0},{2,3},{3,2},{4,5},{5,4},{6,7},{7,6},{8,9},{9,8},{10,11... | collective-permute-start | bytes 2457608 | tf_op jit(solution)/shard_map/ppermute | solution.py:110
  137.9 33.4 %collective-permute-start.8 = (bf16[2,2,2,400,256]{4,3,0,1,2:T(8,128)(2,1)}, bf16[2,2,2,400,256]{4,3,0,1,2:T(8,128)(2,1)}, u32[]{:S(2)}, u32[]{:S(2)}) collective-permute-start(bf16[2,2,2,400,256]{4,3,0,1,2:T(8,128)(2,1)} %copy_bitcast_fusion.3), channel_id=1, source_target_pairs={{0,1},{1,0},{2,3},{3,2},{4,5},{5,4},{6,7},{7,6},{8,9},{9,8},{10,11... | collective-permute-start | bytes 4915208 | tf_op jit(solution)/shard_map/ppermute | solution.py:110
  140.7 33.1 %collective-permute-start.9 = (bf16[2,2,2,400,256]{4,3,0,1,2:T(8,128)(2,1)}, bf16[2,2,2,400,256]{4,3,0,1,2:T(8,128)(2,1)}, u32[]{:S(2)}, u32[]{:S(2)}) collective-permute-start(bf16[2,2,2,400,256]{4,3,0,1,2:T(8,128)(2,1)} %copy_bitcast_fusion.2), channel_id=1, source_target_pairs={{0,2},{1,3},{2,0},{3,1},{4,6},{5,7},{6,4},{7,5},{8,10},{9,11},{10,... | collective-permute-start | bytes 4915208 | tf_op jit(solution)/shard_map/ppermute | solution.py:110
  144.1 14.1 %collective-permute-start.6 = (bf16[2,400,256]{2,1,0:T(8,128)(2,1)}, bf16[2,400,256]{2,1,0:T(8,128)(2,1)}, u32[]{:S(2)}, u32[]{:S(2)}) collective-permute-start(bf16[2,400,256]{2,1,0:T(8,128)(2,1)} %fusion.24), channel_id=1, source_target_pairs={{0,4},{1,5},{2,6},{3,7},{4,0},{5,1},{6,2},{7,3},{8,12},{9,13},{10,... | collective-permute-start | bytes 1228808 | tf_op jit(solution)/shard_map/ppermute | solution.py:110
  149.8 12.9 %collective-permute-start.7 = (bf16[2,400,256]{2,1,0:T(8,128)(2,1)}, bf16[2,400,256]{2,1,0:T(8,128)(2,1)}, u32[]{:S(2)}, u32[]{:S(2)}) collective-permute-start(bf16[2,400,256]{2,1,0:T(8,128)(2,1)} %fusion.25), channel_id=1, source_target_pairs={{0,4},{1,5},{2,6},{3,7},{4,0},{5,1},{6,2},{7,3},{8,12},{9,13},{10,... | collective-permute-start | bytes 1228808 | tf_op jit(solution)/shard_map/ppermute | solution.py:110
  149.8 21.5 %copy-start.1 = (bf16[1,6400,256]{2,1,0:T(8,128)(2,1)S(1)}, bf16[1,6400,256]{2,1,0:T(8,128)(2,1)}, u32[]{:S(2)}) copy-start(bf16[1,6400,256]{2,1,0:T(8,128)(2,1)} %copy-done) | copy-start | bytes 9830404
  159.6 26.1 %copy-start.7 = (f32[2,400,256]{2,1,0:T(8,128)}, f32[2,400,256]{2,1,0:T(8,128)S(1)}, u32[]{:S(2)}) copy-start(f32[2,400,256]{2,1,0:T(8,128)S(1)} %bitcast_add_fusion.7) | copy-start | bytes 2457604
  164.0 14.9 %copy-start.8 = (f32[2,400,256]{2,1,0:T(8,128)}, f32[2,400,256]{2,1,0:T(8,128)S(1)}, u32[]{:S(2)}) copy-start(f32[2,400,256]{2,1,0:T(8,128)S(1)} %bitcast_add_fusion.6) | copy-start | bytes 2457604
  173.1 2.9 copy-start.4
  176.0 11.5 %copy-start.2 = (f32[2,2,2,400,256]{4,3,0,1,2:T(8,128)}, f32[2,2,2,400,256]{4,3,0,1,2:T(8,128)S(1)}, u32[]{:S(2)}) copy-start(f32[2,2,2,400,256]{4,3,0,1,2:T(8,128)S(1)} %convert_add_fusion) | copy-start | bytes 9830404
  177.1 24.9 %collective-permute-start.12 = (bf16[2,2,400,256]{3,2,0,1:T(8,128)(2,1)}, bf16[2,2,400,256]{3,2,0,1:T(8,128)(2,1)}, u32[]{:S(2)}, u32[]{:S(2)}) collective-permute-start(bf16[2,2,400,256]{3,2,0,1:T(8,128)(2,1)} %fusion.20), channel_id=1, source_target_pairs={{0,2},{1,3},{2,0},{3,1},{4,6},{5,7},{6,4},{7,5},{8,10},{9,11},{10,... | collective-permute-start | bytes 2457608 | tf_op jit(solution)/shard_map/ppermute | solution.py:110
  179.6 16.8 %collective-permute-start.11 = (bf16[400,256]{1,0:T(8,128)(2,1)}, bf16[400,256]{1,0:T(8,128)(2,1)}, u32[]{:S(2)}, u32[]{:S(2)}) collective-permute-start(bf16[400,256]{1,0:T(8,128)(2,1)} %fusion.34), channel_id=1, source_target_pairs={{0,8},{1,9},{2,10},{3,11},{4,12},{5,13},{6,14},{7,15},{8,0},{9,1},... | collective-permute-start | bytes 614408 | tf_op jit(solution)/shard_map/ppermute | solution.py:110
  186.5 15.6 %copy-start.5 = (f32[2,2,2,400,256]{4,3,0,1,2:T(8,128)S(1)}, f32[2,2,2,400,256]{4,3,0,1,2:T(8,128)}, u32[]{:S(2)}) copy-start(f32[2,2,2,400,256]{4,3,0,1,2:T(8,128)} %copy-done.4) | copy-start | bytes 9830404
  186.5 14.1 %collective-permute-start.10 = (bf16[400,256]{1,0:T(8,128)(2,1)}, bf16[400,256]{1,0:T(8,128)(2,1)}, u32[]{:S(2)}, u32[]{:S(2)}) collective-permute-start(bf16[400,256]{1,0:T(8,128)(2,1)} %fusion.33), channel_id=1, source_target_pairs={{0,8},{1,9},{2,10},{3,11},{4,12},{5,13},{6,14},{7,15},{8,0},{9,1},... | collective-permute-start | bytes 614408 | tf_op jit(solution)/shard_map/ppermute | solution.py:110
  187.5 16.3 %collective-permute-start.13 = (bf16[2,2,400,256]{3,2,0,1:T(8,128)(2,1)}, bf16[2,2,400,256]{3,2,0,1:T(8,128)(2,1)}, u32[]{:S(2)}, u32[]{:S(2)}) collective-permute-start(bf16[2,2,400,256]{3,2,0,1:T(8,128)(2,1)} %fusion.21), channel_id=1, source_target_pairs={{0,1},{1,0},{2,3},{3,2},{4,5},{5,4},{6,7},{7,6},{8,9},{9,8},{10,11... | collective-permute-start | bytes 2457608 | tf_op jit(solution)/shard_map/ppermute | solution.py:110
  202.1 2.2 copy-start.3
  205.6 8.6 %collective-permute-start.14 = (bf16[400,128]{1,0:T(8,128)(2,1)S(1)}, bf16[400,128]{1,0:T(8,128)(2,1)S(1)}, u32[]{:S(2)}, u32[]{:S(2)}) collective-permute-start(bf16[400,128]{1,0:T(8,128)(2,1)S(1)} %get-tuple-element.61), channel_id=1, source_target_pairs={{0,8},{1,9},{2,10},{3,11},{4,12},{5,13},{6,14},{7,15},{8,0},{9,1},... | collective-permute-start | bytes 307208 | tf_op jit(solution)/shard_map/ppermute | solution.py:117
  207.9 7.9 %collective-permute-start.15 = (bf16[400,128]{1,0:T(8,128)(2,1)S(1)}, bf16[400,128]{1,0:T(8,128)(2,1)S(1)}, u32[]{:S(2)}, u32[]{:S(2)}) collective-permute-start(bf16[400,128]{1,0:T(8,128)(2,1)S(1)} %get-tuple-element.62), channel_id=1, source_target_pairs={{0,8},{1,9},{2,10},{3,11},{4,12},{5,13},{6,14},{7,15},{8,0},{9,1},... | collective-permute-start | bytes 307208 | tf_op jit(solution)/shard_map/ppermute | solution.py:117
  208.6 15.2 %collective-permute-start.16 = (bf16[2,400,256]{2,1,0:T(8,128)(2,1)S(1)}, bf16[2,400,256]{2,1,0:T(8,128)(2,1)S(1)}, u32[]{:S(2)}, u32[]{:S(2)}) collective-permute-start(bf16[2,400,256]{2,1,0:T(8,128)(2,1)S(1)} %fusion.26), channel_id=1, source_target_pairs={{0,4},{1,5},{2,6},{3,7},{4,0},{5,1},{6,2},{7,3},{8,12},{9,13},{10,... | collective-permute-start | bytes 1228808 | tf_op jit(solution)/shard_map/ppermute | solution.py:110
  208.9 23.0 %collective-permute-start.17 = (bf16[2,400,256]{2,1,0:T(8,128)(2,1)S(1)}, bf16[2,400,256]{2,1,0:T(8,128)(2,1)S(1)}, u32[]{:S(2)}, u32[]{:S(2)}) collective-permute-start(bf16[2,400,256]{2,1,0:T(8,128)(2,1)S(1)} %fusion.27), channel_id=1, source_target_pairs={{0,4},{1,5},{2,6},{3,7},{4,0},{5,1},{6,2},{7,3},{8,12},{9,13},{10,... | collective-permute-start | bytes 1228808 | tf_op jit(solution)/shard_map/ppermute | solution.py:110
  232.0 10.8 %collective-permute-start.18 = (bf16[2,400,128]{2,1,0:T(8,128)(2,1)S(1)}, bf16[2,400,128]{2,1,0:T(8,128)(2,1)S(1)}, u32[]{:S(2)}, u32[]{:S(2)}) collective-permute-start(bf16[2,400,128]{2,1,0:T(8,128)(2,1)S(1)} %pad_maximum_fusion.14), channel_id=1, source_target_pairs={{0,4},{1,5},{2,6},{3,7},{4,0},{5,1},{6,2},{7,3},{8,12},{9,13},{10,... | collective-permute-start | bytes 614408 | tf_op jit(solution)/shard_map/ppermute | solution.py:117
  232.1 23.2 %collective-permute-start.19 = (bf16[2,400,128]{2,1,0:T(8,128)(2,1)S(1)}, bf16[2,400,128]{2,1,0:T(8,128)(2,1)S(1)}, u32[]{:S(2)}, u32[]{:S(2)}) collective-permute-start(bf16[2,400,128]{2,1,0:T(8,128)(2,1)S(1)} %pad_maximum_fusion.15), channel_id=1, source_target_pairs={{0,4},{1,5},{2,6},{3,7},{4,0},{5,1},{6,2},{7,3},{8,12},{9,13},{10,... | collective-permute-start | bytes 614408 | tf_op jit(solution)/shard_map/ppermute | solution.py:117
  234.1 17.7 %collective-permute-start.21 = (bf16[400,256]{1,0:T(8,128)(2,1)S(1)}, bf16[400,256]{1,0:T(8,128)(2,1)S(1)}, u32[]{:S(2)}, u32[]{:S(2)}) collective-permute-start(bf16[400,256]{1,0:T(8,128)(2,1)S(1)} %fusion.36), channel_id=1, source_target_pairs={{0,8},{1,9},{2,10},{3,11},{4,12},{5,13},{6,14},{7,15},{8,0},{9,1},... | collective-permute-start | bytes 614408 | tf_op jit(solution)/shard_map/ppermute | solution.py:110
  234.2 20.8 %collective-permute-start.20 = (bf16[400,256]{1,0:T(8,128)(2,1)S(1)}, bf16[400,256]{1,0:T(8,128)(2,1)S(1)}, u32[]{:S(2)}, u32[]{:S(2)}) collective-permute-start(bf16[400,256]{1,0:T(8,128)(2,1)S(1)} %fusion.35), channel_id=1, source_target_pairs={{0,8},{1,9},{2,10},{3,11},{4,12},{5,13},{6,14},{7,15},{8,0},{9,1},... | collective-permute-start | bytes 614408 | tf_op jit(solution)/shard_map/ppermute | solution.py:110
  255.3 7.0 %collective-permute-start.24 = (bf16[400,128]{1,0:T(8,128)(2,1)S(1)}, bf16[400,128]{1,0:T(8,128)(2,1)S(1)}, u32[]{:S(2)}, u32[]{:S(2)}) collective-permute-start(bf16[400,128]{1,0:T(8,128)(2,1)S(1)} %get-tuple-element.71), channel_id=1, source_target_pairs={{0,8},{1,9},{2,10},{3,11},{4,12},{5,13},{6,14},{7,15},{8,0},{9,1},... | collective-permute-start | bytes 307208 | tf_op jit(solution)/shard_map/ppermute | solution.py:117
  255.4 10.4 %collective-permute-start.22 = (bf16[2,2,400,128]{3,2,0,1:T(8,128)(2,1)S(1)}, bf16[2,2,400,128]{3,2,0,1:T(8,128)(2,1)S(1)}, u32[]{:S(2)}, u32[]{:S(2)}) collective-permute-start(bf16[2,2,400,128]{3,2,0,1:T(8,128)(2,1)S(1)} %pad_maximum_fusion.10), channel_id=1, source_target_pairs={{0,2},{1,3},{2,0},{3,1},{4,6},{5,7},{6,4},{7,5},{8,10},{9,11},{10,... | collective-permute-start | bytes 1228808 | tf_op jit(solution)/shard_map/ppermute | solution.py:117
  255.5 10.5 %collective-permute-start.23 = (bf16[2,2,400,128]{3,2,1,0:T(8,128)(2,1)S(1)}, bf16[2,2,400,128]{3,2,1,0:T(8,128)(2,1)S(1)}, u32[]{:S(2)}, u32[]{:S(2)}) collective-permute-start(bf16[2,2,400,128]{3,2,1,0:T(8,128)(2,1)S(1)} %pad_maximum_fusion.11), channel_id=1, source_target_pairs={{0,1},{1,0},{2,3},{3,2},{4,5},{5,4},{6,7},{7,6},{8,9},{9,8},{10,11... | collective-permute-start | bytes 1228808 | tf_op jit(solution)/shard_map/ppermute | solution.py:117
  255.9 7.6 %collective-permute-start.25 = (bf16[400,128]{1,0:T(8,128)(2,1)S(1)}, bf16[400,128]{1,0:T(8,128)(2,1)S(1)}, u32[]{:S(2)}, u32[]{:S(2)}) collective-permute-start(bf16[400,128]{1,0:T(8,128)(2,1)S(1)} %get-tuple-element.72), channel_id=1, source_target_pairs={{0,8},{1,9},{2,10},{3,11},{4,12},{5,13},{6,14},{7,15},{8,0},{9,1},... | collective-permute-start | bytes 307208 | tf_op jit(solution)/shard_map/ppermute | solution.py:117
  266.1 6.6 %collective-permute-start.28 = (bf16[2,400,128]{2,1,0:T(8,128)(2,1)S(1)}, bf16[2,400,128]{2,1,0:T(8,128)(2,1)S(1)}, u32[]{:S(2)}, u32[]{:S(2)}) collective-permute-start(bf16[2,400,128]{2,1,0:T(8,128)(2,1)S(1)} %pad_maximum_fusion.16), channel_id=1, source_target_pairs={{0,4},{1,5},{2,6},{3,7},{4,0},{5,1},{6,2},{7,3},{8,12},{9,13},{10,... | collective-permute-start | bytes 614408 | tf_op jit(solution)/shard_map/ppermute | solution.py:117
  266.2 18.3 %collective-permute-start.26 = (bf16[2,2,2,400,128]{4,3,0,1,2:T(8,128)(2,1)S(1)}, bf16[2,2,2,400,128]{4,3,0,1,2:T(8,128)(2,1)S(1)}, u32[]{:S(2)}, u32[]{:S(2)}) collective-permute-start(bf16[2,2,2,400,128]{4,3,0,1,2:T(8,128)(2,1)S(1)} %pad_maximum_fusion.4), channel_id=1, source_target_pairs={{0,1},{1,0},{2,3},{3,2},{4,5},{5,4},{6,7},{7,6},{8,9},{9,8},{10,11... | collective-permute-start | bytes 2457608 | tf_op jit(solution)/shard_map/ppermute | solution.py:117
  266.5 62.0 %collective-permute-start.34 = (bf16[16,224,512]{2,1,0:T(8,128)(2,1)}, bf16[16,224,512]{2,1,0:T(8,128)(2,1)}, u32[]{:S(2)}, u32[]{:S(2)}) collective-permute-start(bf16[16,224,512]{2,1,0:T(8,128)(2,1)} %get-tuple-element.89), channel_id=1, source_target_pairs={{0,16},{16,0},{1,17},{17,1},{2,18},{18,2},{3,19},{19,3},{4,20},{20... | collective-permute-start | bytes 11010056 | tf_op jit(solution)/shard_map/ppermute | solution.py:168
  266.5 20.7 %collective-permute-start.27 = (bf16[2,2,2,400,128]{4,3,2,1,0:T(8,128)(2,1)S(1)}, bf16[2,2,2,400,128]{4,3,2,1,0:T(8,128)(2,1)S(1)}, u32[]{:S(2)}, u32[]{:S(2)}) collective-permute-start(bf16[2,2,2,400,128]{4,3,2,1,0:T(8,128)(2,1)S(1)} %pad_maximum_fusion.5), channel_id=1, source_target_pairs={{0,2},{1,3},{2,0},{3,1},{4,6},{5,7},{6,4},{7,5},{8,10},{9,11},{10,... | collective-permute-start | bytes 2457608 | tf_op jit(solution)/shard_map/ppermute | solution.py:117
  268.1 8.2 %collective-permute-start.29 = (bf16[2,400,128]{2,1,0:T(8,128)(2,1)S(1)}, bf16[2,400,128]{2,1,0:T(8,128)(2,1)S(1)}, u32[]{:S(2)}, u32[]{:S(2)}) collective-permute-start(bf16[2,400,128]{2,1,0:T(8,128)(2,1)S(1)} %pad_maximum_fusion.17), channel_id=1, source_target_pairs={{0,4},{1,5},{2,6},{3,7},{4,0},{5,1},{6,2},{7,3},{8,12},{9,13},{10,... | collective-permute-start | bytes 614408 | tf_op jit(solution)/shard_map/ppermute | solution.py:117
  287.4 11.2 %collective-permute-start.30 = (bf16[2,2,400,128]{3,2,0,1:T(8,128)(2,1)S(1)}, bf16[2,2,400,128]{3,2,0,1:T(8,128)(2,1)S(1)}, u32[]{:S(2)}, u32[]{:S(2)}) collective-permute-start(bf16[2,2,400,128]{3,2,0,1:T(8,128)(2,1)S(1)} %pad_maximum_fusion.12), channel_id=1, source_target_pairs={{0,2},{1,3},{2,0},{3,1},{4,6},{5,7},{6,4},{7,5},{8,10},{9,11},{10,... | collective-permute-start | bytes 1228808 | tf_op jit(solution)/shard_map/ppermute | solution.py:117
  289.1 10.8 %collective-permute-start.31 = (bf16[2,2,400,128]{3,2,1,0:T(8,128)(2,1)S(1)}, bf16[2,2,400,128]{3,2,1,0:T(8,128)(2,1)S(1)}, u32[]{:S(2)}, u32[]{:S(2)}) collective-permute-start(bf16[2,2,400,128]{3,2,1,0:T(8,128)(2,1)S(1)} %pad_maximum_fusion.13), channel_id=1, source_target_pairs={{0,1},{1,0},{2,3},{3,2},{4,5},{5,4},{6,7},{7,6},{8,9},{9,8},{10,11... | collective-permute-start | bytes 1228808 | tf_op jit(solution)/shard_map/ppermute | solution.py:117
  301.0 19.0 %collective-permute-start.32 = (bf16[2,2,2,400,128]{4,3,0,1,2:T(8,128)(2,1)}, bf16[2,2,2,400,128]{4,3,0,1,2:T(8,128)(2,1)}, u32[]{:S(2)}, u32[]{:S(2)}) collective-permute-start(bf16[2,2,2,400,128]{4,3,0,1,2:T(8,128)(2,1)} %pad_maximum_fusion.6), channel_id=1, source_target_pairs={{0,1},{1,0},{2,3},{3,2},{4,5},{5,4},{6,7},{7,6},{8,9},{9,8},{10,11... | collective-permute-start | bytes 2457608 | tf_op jit(solution)/shard_map/ppermute | solution.py:117
  302.7 19.0 %collective-permute-start.33 = (bf16[2,2,2,400,128]{4,3,2,1,0:T(8,128)(2,1)}, bf16[2,2,2,400,128]{4,3,2,1,0:T(8,128)(2,1)}, u32[]{:S(2)}, u32[]{:S(2)}) collective-permute-start(bf16[2,2,2,400,128]{4,3,2,1,0:T(8,128)(2,1)} %pad_maximum_fusion.7), channel_id=1, source_target_pairs={{0,2},{1,3},{2,0},{3,1},{4,6},{5,7},{6,4},{7,5},{8,10},{9,11},{10,... | collective-permute-start | bytes 2457608 | tf_op jit(solution)/shard_map/ppermute | solution.py:117
  362.8 4.0 %copy-start.9 = (f32[2,768,224]{2,1,0:T(8,128)S(1)}, f32[2,768,224]{2,1,0:T(8,128)}, u32[]{:S(2)}) copy-start(f32[2,768,224]{2,1,0:T(8,128)} %shard_map.66) | copy-start | bytes 4128772
  363.0 2.3 collective-permute-start.35

commit v4 on v3

--- a/solution.py
+++ b/solution.py
@@ -41,17 +41,22 @@
 
 def up_kernel(parts, fresh, starts, chunks, order, mine, *refs):
     if fresh:
-        slots_ref, x_ref, weights, (out_ref, packed_ref) = refs[0], refs[1], refs[2:-2], refs[-2:]
+        slots_ref, x_ref, weights, (a_ref, b_ref, packed_ref) = refs[0], refs[1], refs[2:-3], refs[-3:]
     else:
-        packed_ref, weights, out_ref = refs[0], refs[1:-1], refs[-1]
+        packed_ref, weights, (a_ref, b_ref) = refs[0], refs[1:-2], refs[-2:]
     e = pl.program_id(0)
+    total = a_ref.shape[0]
 
     @pl.when(e == 0)
     def _():
-        out_ref[...] = jnp.zeros_like(out_ref)
+        a_ref[...] = jnp.zeros_like(a_ref)
+        b_ref[...] = jnp.zeros_like(b_ref)
 
     def step(c, carry):
-        base = pl.multiple_of(starts[e] + c * TILE, ALIGN)
+        first = starts[e] + c * TILE
+        base = pl.multiple_of(jnp.minimum(first, total - TILE), ALIGN)
+        ours = pl.ds(base, TILE)
+        fits = (base + lax.broadcasted_iota(jnp.int32, (TILE, 1), 0)) >= first
         if fresh:
             slots = slots_ref[0]
             pick = slots == base + lax.broadcasted_iota(jnp.int32, (TILE, slots.shape[1]), 0)
@@ -59,15 +64,16 @@
         a = b = None
         for i in range(parts):
             if fresh:
-                xs = dot(pick, x_ref[i]).astype(BF16)
-                packed_ref[i, pl.ds(base, TILE), :] = xs
+                xs = dot(pick, x_ref[i])
+                xs = jnp.where(fits, xs, packed_ref[i, ours, :].astype(F32)).astype(BF16)
+                packed_ref[i, ours, :] = xs
             else:
-                xs = packed_ref[i, pl.ds(base, TILE), :]
+                xs = packed_ref[i, ours, :]
             da = dot(xs, weights[2 * i][0])
             db = dot(xs, weights[2 * i + 1][0])
             a, b = (da, db) if a is None else (a + da, b + db)
-        out_ref[0, pl.ds(base, TILE), :] = a.astype(out_ref.dtype)
-        out_ref[1, pl.ds(base, TILE), :] = b.astype(out_ref.dtype)
+        a_ref[ours, :] = jnp.where(fits, a, a_ref[ours, :].astype(F32)).astype(BF16)
+        b_ref[ours, :] = jnp.where(fits, b, b_ref[ours, :].astype(F32)).astype(BF16)
         return carry
 
     lax.fori_loop(0, chunks[e], step, 0)
@@ -105,8 +111,9 @@
 def halve(cur, left, b, n):
     axis = left.index(b)
     bit = (lax.axis_index("expert") >> b) & 1
-    send = lax.dynamic_index_in_dim(cur, 1 - bit, axis, keepdims=False).astype(BF16)
-    keep = lax.dynamic_index_in_dim(cur, bit, axis, keepdims=False).astype(F32)
+    low, high = (lax.index_in_dim(cur, i, axis, keepdims=False) for i in range(2))
+    send = jnp.where(bit == 1, low, high).astype(BF16)
+    keep = jnp.where(bit == 1, high, low).astype(F32)
     got = lax.ppermute(send, "expert", [(i, i ^ (1 << b)) for i in range(n)])
     return keep + got.astype(F32), [i for i in left if i != b]
 
@@ -201,25 +208,24 @@
         for got in others:
             specs += [other(cols, q)] * 2
             args += got[:2]
-        ab_shape = (2, packed + TILE, cols)
-        xs_shape = (parts, packed + TILE, local)
+        ab_shape = (packed, cols)
+        xs_shape = (parts, packed, local)
         fresh = q == 0
         made = pl.pallas_call(
             functools.partial(up_kernel, parts, fresh),
-            out_shape=[jax.ShapeDtypeStruct(i, BF16) for i in ([ab_shape, xs_shape] if fresh else [ab_shape])],
+            out_shape=[jax.ShapeDtypeStruct(i, BF16) for i in ([ab_shape] * 2 + [xs_shape] * fresh)],
             grid_spec=pltpu.PrefetchScalarGridSpec(
                 num_scalar_prefetch=4,
                 grid=(experts,),
                 in_specs=([line, whole(parts, rows, local)] if fresh else [whole(*xs_shape)]) + specs,
-                out_specs=[whole(*i) for i in ([ab_shape, xs_shape] if fresh else [ab_shape])],
+                out_specs=[whole(*i) for i in ([ab_shape] * 2 + [xs_shape] * fresh)],
             ),
             compiler_params=params,
             cost_estimate=pl.CostEstimate(flops=2 * 10**10, bytes_accessed=5 * 10**7, transcendentals=0),
         )(*scalars, *([slots, x] if fresh else [xs]), *args)
         if fresh:
-            xs = made[1]
-        ab = made[0]
-        pieces.append([ab[0, :packed], ab[1, :packed]])
+            xs = made[2]
+        pieces.append(made[:2])
     hs = exchange_all(pieces, owners)
     down_specs, down_args = [own(2, share, 0)], [expert_weights]
     for got in others:

time: 391 us -> 386 us (0.987)
  local copies, waits for them, and re-layouts: 43.3 us -> 26.3 us
  other arithmetic: 29.1 us -> 35.2 us
  waiting for transfers between devices: 163 us -> 168 us
    convert_element_type x12 -> x0, local copies, waits for them, and re-layouts: 7.71 us -> none  [halve(): lax.dynamic_index_in_dim(cur, 1 - bit, axis, keepdims=False).astype(BF16)]
    select_n x0 -> x4, other arithmetic: none -> 6.15 us  [halve(): send = jnp.where(bit == 1, low, high).astype(BF16)]
    ppermute x16, waiting for transfers between devices: 83.4 us -> 88.9 us  [halve(): got = lax.ppermute(send, 'expert', [(i, i ^ 1 << b) for i in range(n)])]
    slice x2, local copies, waits for them, and re-layouts: 6.69 us -> 2.35 us  [halve(): lax.index_in_dim(cur, i, axis, keepdims=False)]
    dynamic_slice x4 -> x0, local copies, waits for them, and re-layouts: 4.27 us -> none  [the longest x2 2.64 us: halve(): lax.dynamic_index_in_dim(cur, 1 - bit, axis, keepdims=False).astype(BF16)]
  transfers between devices with their start and end apart: 37 -> 37, of which waited for: 30 -> 31; matrix products, arithmetic and copies ran while one was open for 12% -> 9% of each run, Pallas kernels for 5% -> 5%
where the time goes in v4:
time: 386 us; the launch traced here: 384 us
  waiting for transfers between devices  168 us (44%)
  Pallas kernels  80.9 us (21%)
  starting transfers between devices  52.6 us (14%)
  other arithmetic  35.2 us (9%)
  local copies, waits for them, and re-layouts  26.3 us (7%)
  blocking collectives  19.9 us (5%)
    ppermute x16, waiting for transfers between devices, halve(): got = lax.ppermute(send, 'expert', [(i, i ^ 1 << b) for i in range(n)])  88.9 us
    ppermute x16, waiting for transfers between devices, double(): got = lax.ppermute(cur, 'expert', [(i, i ^ 1 << b) for i in range(n)])  56.6 us
    pallas_call x2, Pallas kernels, body(): pl.pallas_call(functools.partial(up_kernel, parts, fresh), out_shape=[jax...  46.6 us
    pallas_call x1, Pallas kernels, body(): pl.pallas_call(functools.partial(down_kernel, parts), out_shape=jax.Shape...  34.3 us
    ppermute x16, starting transfers between devices, halve(): got = lax.ppermute(send, 'expert', [(i, i ^ 1 << b) for i in range(n)])  24.3 us
    all_to_all x1, blocking collectives, body(): y = lax.all_to_all(y, 'expert', split_axis=1, concat_axis=1, tiled=True)  19.9 us
    all_to_all x1, waiting for transfers between devices, body(): x = lax.all_to_all(x, 'expert', split_axis=0, concat_axis=0, tiled=True)  19.8 us
    ppermute x16, starting transfers between devices, double(): got = lax.ppermute(cur, 'expert', [(i, i ^ 1 << b) for i in range(n)])  19.4 us
  transfers between devices with their start and end apart: 37, of which 31 were waited for; matrix products, arithmetic and copies ran while one was open for 9% of the time, Pallas kernels for 5%

profile of v4, /device:TPU:0, one launch (start us, length us, event | category | flops | bytes accessed | tf_op | source)
XLA Modules:
  0.0 384.1 jit_solution(1819222934484742507)
XLA Ops:
  0.0 8.9 %constant_dynamic-slice_fusion.2 = (bf16[16,224,512]{2,1,0:T(8,128)(2,1)}, bf16[16,224,512]{2,1,0:T(8,128)(2,1)}, bf16[16,224,512]{2,1,0:T(8,128)(2,1)}) fusion(bf16[16,224,3072]{2,1,0:T(8,128)(2,1)} %refs_4_.1, s32[]{:T(128)S(6)} %select_n.544, s32[]{:T(128)S(6)} %select_n.459, s32[]{:T(128)S(6)} %select_n.458), kind=kLoop, calls=%fused_computation.137 | loop fusion | bytes 22020108 | tf_op jit(solution)/shard_map/dynamic_slice | solution.py:172
  13.1 8.3 %all-to-all-start = ((bf16[16,3,16,464]{3,2,1,0:T(8,128)(2,1)}), bf16[16,3,16,464]{3,2,1,0:T(8,128)(2,1)S(1)}, u32[]{:S(2)}, u32[]{:S(2)}) async-start(bf16[16,3,16,464]{3,2,1,0:T(8,128)(2,1)} %pad_maximum_fusion.8), calls=%async_computation | async-start | bytes 1572864 | tf_op jit(solution)/shard_map/all_to_all | solution.py:182
  21.5 19.8 %all-to-all-done = bf16[16,3,16,464]{3,2,1,0:T(8,128)(2,1)S(1)} async-done(((bf16[16,3,16,464]{3,2,1,0:T(8,128)(2,1)}), bf16[16,3,16,464]{3,2,1,0:T(8,128)(2,1)S(1)}, u32[]{:S(2)}, u32[]{:S(2)}) %all-to-all-start) | async-done | bytes 712736 | tf_op jit(solution)/shard_map/all_to_all | solution.py:182
  46.1 26.7 %shard_map.64 = (bf16[6400,256]{1,0:T(8,128)(2,1)}, bf16[6400,256]{1,0:T(8,128)(2,1)}, bf16[2,6400,224]{2,1,0:T(8,128)(2,1)}) custom-call(s32[16]{0:T(128)} %copy-done.14, s32[16]{0:T(128)} %get-tuple-element.142.chunks, s32[16]{0:T(128)} %get-tuple-element.146.order, s32[1]{0:T(128)} %bitcast.3.mine, s32[16,1,768]{2,1,0:T(1,128)} %broadcast_in_dim.63.refs_0_.slots_ref, ...), custom_call_target="tpu_custom_call" | custom-call | flops 20000000000 | bytes 50000000 | tf_op jit(solution)/shard_map/pallas_call | solution.py:214
  72.8 2.1 fusion.42
  74.9 1.3 select_bitcast_fusion.3
  77.7 1.6 select_bitcast_fusion.2
  79.5 1.6 collective-permute-start.3
  81.1 19.9 %shard_map.65 = (bf16[6400,256]{1,0:T(8,128)(2,1)}, bf16[6400,256]{1,0:T(8,128)(2,1)}) custom-call(s32[16]{0:T(128)} %copy-done.14, s32[16]{0:T(128)} %get-tuple-element.142.chunks, s32[16]{0:T(128)} %get-tuple-element.146.order, s32[1]{0:T(128)} %bitcast.3.mine, bf16[2,6400,224]{2,1,0:T(8,128)(2,1)} %get-tuple-element.52.refs_0_, ...), custom_call_target="tpu_custom_call" | custom-call | flops 20000000000 | bytes 50000000 | tf_op jit(solution)/shard_map/pallas_call | solution.py:214
  101.0 10.2 %collective-permute-done.2 = bf16[2,2,2,400,256]{4,3,0,1,2:T(8,128)(2,1)} collective-permute-done((bf16[2,2,2,400,256]{4,3,0,1,2:T(8,128)(2,1)}, bf16[2,2,2,400,256]{4,3,0,1,2:T(8,128)(2,1)}, u32[]{:S(2)}, u32[]{:S(2)}) %collective-permute-start.2) | collective-permute-done | bytes 1638432 | tf_op jit(solution)/shard_map/ppermute | solution.py:117
  111.2 2.0 convert_add_fusion.3
  113.2 1.9 collective-permute-done.3
  115.1 2.0 convert_add_fusion.2
  117.2 1.8 collective-permute-start.4
  119.8 14.4 %collective-permute-done.4 = bf16[2,2,400,256]{3,2,0,1:T(8,128)(2,1)S(1)} collective-permute-done((bf16[2,2,400,256]{3,2,0,1:T(8,128)(2,1)S(1)}, bf16[2,2,400,256]{3,2,0,1:T(8,128)(2,1)S(1)}, u32[]{:S(2)}, u32[]{:S(2)}) %collective-permute-start.4) | collective-permute-done | bytes 819232 | tf_op jit(solution)/shard_map/ppermute | solution.py:117
  134.3 1.5 bitcast_add_fusion.3
  135.9 1.5 bitcast_add_fusion.2
  138.3 1.7 select_bitcast_fusion.1
  140.8 1.6 select_bitcast_fusion
  142.3 1.7 collective-permute-start.9
  144.9 3.7 collective-permute-start.6
  149.4 9.9 %collective-permute-done.6 = bf16[2,400,256]{2,1,0:T(8,128)(2,1)} collective-permute-done((bf16[2,400,256]{2,1,0:T(8,128)(2,1)}, bf16[2,400,256]{2,1,0:T(8,128)(2,1)}, u32[]{:S(2)}, u32[]{:S(2)}) %collective-permute-start.6) | collective-permute-done | bytes 409632 | tf_op jit(solution)/shard_map/ppermute | solution.py:117
  159.3 1.8 bitcast_add_fusion.7
  161.1 2.9 collective-permute-done.7
  165.1 8.7 %collective-permute-done.8 = bf16[2,2,2,400,256]{4,3,0,1,2:T(8,128)(2,1)} collective-permute-done((bf16[2,2,2,400,256]{4,3,0,1,2:T(8,128)(2,1)}, bf16[2,2,2,400,256]{4,3,0,1,2:T(8,128)(2,1)}, u32[]{:S(2)}, u32[]{:S(2)}) %collective-permute-start.8) | collective-permute-done | bytes 1638432 | tf_op jit(solution)/shard_map/ppermute | solution.py:117
  173.8 2.0 convert_add_fusion.1
  176.2 2.0 convert_add_fusion
  178.3 6.5 %collective-permute-start.11 = (bf16[400,256]{1,0:T(8,128)(2,1)S(1)}, bf16[400,256]{1,0:T(8,128)(2,1)S(1)}, u32[]{:S(2)}, u32[]{:S(2)}) collective-permute-start(bf16[400,256]{1,0:T(8,128)(2,1)S(1)} %fusion.34), channel_id=1, source_target_pairs={{0,8},{1,9},{2,10},{3,11},{4,12},{5,13},{6,14},{7,15},{8,0},{9,1},... | collective-permute-start | bytes 614408 | tf_op jit(solution)/shard_map/ppermute | solution.py:117
  187.3 8.0 %collective-permute-done.11 = bf16[400,256]{1,0:T(8,128)(2,1)S(1)} collective-permute-done((bf16[400,256]{1,0:T(8,128)(2,1)S(1)}, bf16[400,256]{1,0:T(8,128)(2,1)S(1)}, u32[]{:S(2)}, u32[]{:S(2)}) %collective-permute-start.11) | collective-permute-done | bytes 204832 | tf_op jit(solution)/shard_map/ppermute | solution.py:117
  195.3 4.0 %collective-permute-done.10 = bf16[400,256]{1,0:T(8,128)(2,1)S(1)} collective-permute-done((bf16[400,256]{1,0:T(8,128)(2,1)S(1)}, bf16[400,256]{1,0:T(8,128)(2,1)S(1)}, u32[]{:S(2)}, u32[]{:S(2)}) %collective-permute-start.10) | collective-permute-done | bytes 204832 | tf_op jit(solution)/shard_map/ppermute | solution.py:117
  199.5 1.4 collective-permute-done.12
  202.4 2.7 collective-permute-start.14
  205.5 1.5 collective-permute-start.16
  208.5 3.3 collective-permute-done.15
  211.8 7.2 %collective-permute-done.16 = bf16[2,400,256]{2,1,0:T(8,128)(2,1)S(1)} collective-permute-done((bf16[2,400,256]{2,1,0:T(8,128)(2,1)S(1)}, bf16[2,400,256]{2,1,0:T(8,128)(2,1)S(1)}, u32[]{:S(2)}, u32[]{:S(2)}) %collective-permute-start.16) | collective-permute-done | bytes 409632 | tf_op jit(solution)/shard_map/ppermute | solution.py:117
  219.2 7.1 %collective-permute-done.17 = bf16[2,400,256]{2,1,0:T(8,128)(2,1)S(1)} collective-permute-done((bf16[2,400,256]{2,1,0:T(8,128)(2,1)S(1)}, bf16[2,400,256]{2,1,0:T(8,128)(2,1)S(1)}, u32[]{:S(2)}, u32[]{:S(2)}) %collective-permute-start.17) | collective-permute-done | bytes 409632 | tf_op jit(solution)/shard_map/ppermute | solution.py:117
  226.5 2.0 collective-permute-start.19
  228.7 3.0 collective-permute-start.20
  231.6 6.4 %collective-permute-done.18 = bf16[2,400,128]{2,1,0:T(8,128)(2,1)S(1)} collective-permute-done((bf16[2,400,128]{2,1,0:T(8,128)(2,1)S(1)}, bf16[2,400,128]{2,1,0:T(8,128)(2,1)S(1)}, u32[]{:S(2)}, u32[]{:S(2)}) %collective-permute-start.18) | collective-permute-done | bytes 204832 | tf_op jit(solution)/shard_map/ppermute | solution.py:124
  238.1 8.7 %collective-permute-done.21 = bf16[400,256]{1,0:T(8,128)(2,1)S(1)} collective-permute-done((bf16[400,256]{1,0:T(8,128)(2,1)S(1)}, bf16[400,256]{1,0:T(8,128)(2,1)S(1)}, u32[]{:S(2)}, u32[]{:S(2)}) %collective-permute-start.21) | collective-permute-done | bytes 204832 | tf_op jit(solution)/shard_map/ppermute | solution.py:117
  246.8 2.8 collective-permute-done.20
  251.5 2.8 collective-permute-start.25
  254.4 2.4 collective-permute-done.24
  257.9 2.2 collective-permute-done.22
  261.2 1.4 collective-permute-start.27
  262.6 1.9 collective-permute-start.29
  264.5 2.4 collective-permute-done.28
  267.0 3.7 collective-permute-done.29
  270.8 7.6 %collective-permute-done.26 = bf16[2,2,2,400,128]{4,3,0,1,2:T(8,128)(2,1)S(1)} collective-permute-done((bf16[2,2,2,400,128]{4,3,0,1,2:T(8,128)(2,1)S(1)}, bf16[2,2,2,400,128]{4,3,0,1,2:T(8,128)(2,1)S(1)}, u32[]{:S(2)}, u32[]{:S(2)}) %collective-permute-start.26) | collective-permute-done | bytes 819232 | tf_op jit(solution)/shard_map/ppermute | solution.py:124
  278.7 3.2 collective-permute-done.27
  282.1 1.4 collective-permute-start.30
  283.6 1.6 collective-permute-start.31
  285.2 8.1 %collective-permute-done.30 = bf16[2,2,400,128]{3,2,0,1:T(8,128)(2,1)S(1)} collective-permute-done((bf16[2,2,400,128]{3,2,0,1:T(8,128)(2,1)S(1)}, bf16[2,2,400,128]{3,2,0,1:T(8,128)(2,1)S(1)}, u32[]{:S(2)}, u32[]{:S(2)}) %collective-permute-start.30) | collective-permute-done | bytes 409632 | tf_op jit(solution)/shard_map/ppermute | solution.py:124
  295.4 1.6 collective-permute-start.32
  297.0 1.3 collective-permute-start.33
  299.2 15.5 %collective-permute-done.32 = bf16[2,2,2,400,128]{4,3,0,1,2:T(8,128)(2,1)} collective-permute-done((bf16[2,2,2,400,128]{4,3,0,1,2:T(8,128)(2,1)}, bf16[2,2,2,400,128]{4,3,0,1,2:T(8,128)(2,1)}, u32[]{:S(2)}, u32[]{:S(2)}) %collective-permute-start.32) | collective-permute-done | bytes 819232 | tf_op jit(solution)/shard_map/ppermute | solution.py:124
  314.7 1.5 select_bitcast_fusion.7
  316.4 1.5 select_bitcast_fusion.5
  317.9 1.3 pad_maximum_fusion.3
  323.1 34.3 %shard_map.66 = f32[2,768,224]{2,1,0:T(8,128)} custom-call(s32[16]{0:T(128)} %copy-done.14, s32[16]{0:T(128)} %get-tuple-element.142.chunks, s32[16]{0:T(128)} %get-tuple-element.146.order, s32[1]{0:T(128)} %bitcast.3.mine, s32[16,1,768]{2,1,0:T(1,128)} %broadcast_in_dim.63.refs_0_.slots_ref, f32[16,1,768]{2,1,0:T(1,128)} %broadcast_in_dim.66.gates_ref, ...), custom_call_target="tpu_custom_call" | custom-call | flops 11744051200 | bytes 20000000 | tf_op jit(solution)/shard_map/pallas_call | solution.py:235
  359.0 2.3 collective-permute-done.35
  361.2 1.4 copy.170
  362.8 19.9 %all_to_all.10 = bf16[3,16,16,224]{3,2,0,1:T(8,128)(2,1)S(1)} all-to-all(bf16[3,16,16,224]{3,2,0,1:T(8,128)(2,1)S(1)} %copy.171), channel_id=1, replica_groups=mesh['fsdp'=2,'expert'=16] {'expert'}, dimensions={1} | all-to-all | bytes 688128 | tf_op jit(solution)/shard_map/all_to_all | solution.py:252
  382.8 1.3 reshape.239
  (148 shorter events, 36.6 us)
Async XLA Ops:
  0.0 9.4 %copy-start.11 = (s32[3,16,8]{1,2,0:T(8,128)S(1)}, s32[3,16,8]{1,2,0:T(8,128)}, u32[]{:S(2)}) copy-start(s32[3,16,8]{1,2,0:T(8,128)} %param.7) | copy-start | bytes 4612
  0.0 9.5 %copy-start.12 = (bf16[3,16,8]{1,2,0:T(8,128)(2,1)S(1)}, bf16[3,16,8]{1,2,0:T(8,128)(2,1)}, u32[]{:S(2)}) copy-start(bf16[3,16,8]{1,2,0:T(8,128)(2,1)} %param.8) | copy-start | bytes 2308
  0.0 9.6 %copy-start.10 = (bf16[3,16,7168]{2,1,0:T(8,128)(2,1)S(1)}, bf16[3,16,7168]{2,1,0:T(8,128)(2,1)}, u32[]{:S(2)}) copy-start(bf16[3,16,7168]{2,1,0:T(8,128)(2,1)} %param.6) | copy-start | bytes 2064388
  8.9 37.1 %collective-permute-start = (bf16[16,224,512]{2,1,0:T(8,128)(2,1)}, bf16[16,224,512]{2,1,0:T(8,128)(2,1)}, u32[]{:S(2)}, u32[]{:S(2)}) collective-permute-start(bf16[16,224,512]{2,1,0:T(8,128)(2,1)} %get-tuple-element.97), channel_id=1, source_target_pairs={{0,16},{16,0},{1,17},{17,1},{2,18},{18,2},{3,19},{19,3},{4,20},{20... | collective-permute-start | bytes 11010056 | tf_op jit(solution)/shard_map/ppermute | solution.py:175
  9.4 36.7 %collective-permute-start.1 = (bf16[16,224,512]{2,1,0:T(8,128)(2,1)}, bf16[16,224,512]{2,1,0:T(8,128)(2,1)}, u32[]{:S(2)}, u32[]{:S(2)}) collective-permute-start(bf16[16,224,512]{2,1,0:T(8,128)(2,1)} %get-tuple-element.96), channel_id=1, source_target_pairs={{0,16},{16,0},{1,17},{17,1},{2,18},{18,2},{3,19},{19,3},{4,20},{20... | collective-permute-start | bytes 11010056 | tf_op jit(solution)/shard_map/ppermute | solution.py:175
  13.1 28.2 %all-to-all-start = ((bf16[16,3,16,464]{3,2,1,0:T(8,128)(2,1)}), bf16[16,3,16,464]{3,2,1,0:T(8,128)(2,1)S(1)}, u32[]{:S(2)}, u32[]{:S(2)}) async-start(bf16[16,3,16,464]{3,2,1,0:T(8,128)(2,1)} %pad_maximum_fusion.8), calls=%async_computation | async-start | bytes 1572864 | tf_op jit(solution)/shard_map/all_to_all | solution.py:182
  21.4 20.3 %copy-start.15 = (s32[16]{0:T(128)S(1)}, s32[16]{0:T(128)}, u32[]{:S(2)}) copy-start(s32[16]{0:T(128)} %param.9) | copy-start | bytes 196
  41.4 1.6 copy-start.13
  43.7 2.4 copy-start.14
  74.9 2.5 copy-start.8
  76.3 35.0 %collective-permute-start.2 = (bf16[2,2,2,400,256]{4,3,0,1,2:T(8,128)(2,1)}, bf16[2,2,2,400,256]{4,3,0,1,2:T(8,128)(2,1)}, u32[]{:S(2)}, u32[]{:S(2)}) collective-permute-start(bf16[2,2,2,400,256]{4,3,0,1,2:T(8,128)(2,1)} %select_bitcast_fusion.3), channel_id=1, source_target_pairs={{0,1},{1,0},{2,3},{3,2},{4,5},{5,4},{6,7},{7,6},{8,9},{9,8},{10,11... | collective-permute-start | bytes 4915208 | tf_op jit(solution)/shard_map/ppermute | solution.py:117
  77.7 1.8 copy-start
  79.5 35.6 %collective-permute-start.3 = (bf16[2,2,2,400,256]{4,3,0,1,2:T(8,128)(2,1)}, bf16[2,2,2,400,256]{4,3,0,1,2:T(8,128)(2,1)}, u32[]{:S(2)}, u32[]{:S(2)}) collective-permute-start(bf16[2,2,2,400,256]{4,3,0,1,2:T(8,128)(2,1)} %select_bitcast_fusion.2), channel_id=1, source_target_pairs={{0,2},{1,3},{2,0},{3,1},{4,6},{5,7},{6,4},{7,5},{8,10},{9,11},{10,... | collective-permute-start | bytes 4915208 | tf_op jit(solution)/shard_map/ppermute | solution.py:117
  101.0 14.2 %copy-start.1 = (bf16[2,2,1,2,400,256]{5,4,3,2,1,0:T(8,128)(2,1)S(1)}, bf16[2,2,1,2,400,256]{5,4,3,2,1,0:T(8,128)(2,1)}, u32[]{:S(2)}) copy-start(bf16[2,2,1,2,400,256]{5,4,3,2,1,0:T(8,128)(2,1)} %copy-done) | copy-start | bytes 4915204
  117.2 17.0 %collective-permute-start.4 = (bf16[2,2,400,256]{3,2,0,1:T(8,128)(2,1)S(1)}, bf16[2,2,400,256]{3,2,0,1:T(8,128)(2,1)S(1)}, u32[]{:S(2)}, u32[]{:S(2)}) collective-permute-start(bf16[2,2,400,256]{3,2,0,1:T(8,128)(2,1)S(1)} %fusion.18), channel_id=1, source_target_pairs={{0,2},{1,3},{2,0},{3,1},{4,6},{5,7},{6,4},{7,5},{8,10},{9,11},{10,... | collective-permute-start | bytes 2457608 | tf_op jit(solution)/shard_map/ppermute | solution.py:117
  119.2 16.8 %collective-permute-start.5 = (bf16[2,2,400,256]{3,2,0,1:T(8,128)(2,1)S(1)}, bf16[2,2,400,256]{3,2,0,1:T(8,128)(2,1)S(1)}, u32[]{:S(2)}, u32[]{:S(2)}) collective-permute-start(bf16[2,2,400,256]{3,2,0,1:T(8,128)(2,1)S(1)} %fusion.19), channel_id=1, source_target_pairs={{0,1},{1,0},{2,3},{3,2},{4,5},{5,4},{6,7},{7,6},{8,9},{9,8},{10,11... | collective-permute-start | bytes 2457608 | tf_op jit(solution)/shard_map/ppermute | solution.py:117
  135.7 2.5 copy-start.3
  138.3 2.5 copy-start.2
  139.9 33.9 %collective-permute-start.8 = (bf16[2,2,2,400,256]{4,3,0,1,2:T(8,128)(2,1)}, bf16[2,2,2,400,256]{4,3,0,1,2:T(8,128)(2,1)}, u32[]{:S(2)}, u32[]{:S(2)}) collective-permute-start(bf16[2,2,2,400,256]{4,3,0,1,2:T(8,128)(2,1)} %select_bitcast_fusion.1), channel_id=1, source_target_pairs={{0,1},{1,0},{2,3},{3,2},{4,5},{5,4},{6,7},{7,6},{8,9},{9,8},{10,11... | collective-permute-start | bytes 4915208 | tf_op jit(solution)/shard_map/ppermute | solution.py:117
  140.8 3.3 copy-start.5
  140.8 7.8 %copy-start.6 = (f32[2,2,400,256]{3,2,0,1:T(8,128)S(1)}, f32[2,2,400,256]{3,2,0,1:T(8,128)}, u32[]{:S(2)}) copy-start(f32[2,2,400,256]{3,2,0,1:T(8,128)} %bitcast_add_fusion.2) | copy-start | bytes 4915204
  142.3 33.9 %collective-permute-start.9 = (bf16[2,2,2,400,256]{4,3,0,1,2:T(8,128)(2,1)}, bf16[2,2,2,400,256]{4,3,0,1,2:T(8,128)(2,1)}, u32[]{:S(2)}, u32[]{:S(2)}) collective-permute-start(bf16[2,2,2,400,256]{4,3,0,1,2:T(8,128)(2,1)} %select_bitcast_fusion), channel_id=1, source_target_pairs={{0,2},{1,3},{2,0},{3,1},{4,6},{5,7},{6,4},{7,5},{8,10},{9,11},{10,... | collective-permute-start | bytes 4915208 | tf_op jit(solution)/shard_map/ppermute | solution.py:117
  144.9 14.4 %collective-permute-start.6 = (bf16[2,400,256]{2,1,0:T(8,128)(2,1)}, bf16[2,400,256]{2,1,0:T(8,128)(2,1)}, u32[]{:S(2)}, u32[]{:S(2)}) collective-permute-start(bf16[2,400,256]{2,1,0:T(8,128)(2,1)} %fusion.24), channel_id=1, source_target_pairs={{0,4},{1,5},{2,6},{3,7},{4,0},{5,1},{6,2},{7,3},{8,12},{9,13},{10,... | collective-permute-start | bytes 1228808 | tf_op jit(solution)/shard_map/ppermute | solution.py:117
  149.4 14.6 %collective-permute-start.7 = (bf16[2,400,256]{2,1,0:T(8,128)(2,1)}, bf16[2,400,256]{2,1,0:T(8,128)(2,1)}, u32[]{:S(2)}, u32[]{:S(2)}) collective-permute-start(bf16[2,400,256]{2,1,0:T(8,128)(2,1)} %fusion.25), channel_id=1, source_target_pairs={{0,4},{1,5},{2,6},{3,7},{4,0},{5,1},{6,2},{7,3},{8,12},{9,13},{10,... | collective-permute-start | bytes 1228808 | tf_op jit(solution)/shard_map/ppermute | solution.py:117
  149.4 14.6 %copy-start.7 = (f32[2,2,400,256]{3,2,0,1:T(8,128)S(1)}, f32[2,2,400,256]{3,2,0,1:T(8,128)}, u32[]{:S(2)}) copy-start(f32[2,2,400,256]{3,2,0,1:T(8,128)} %bitcast_add_fusion.2) | copy-start | bytes 4915204
  159.3 14.5 %copy-start.4 = (bf16[6400,256]{1,0:T(8,128)(2,1)S(1)}, bf16[6400,256]{1,0:T(8,128)(2,1)}, u32[]{:S(2)}) copy-start(bf16[6400,256]{1,0:T(8,128)(2,1)} %get-tuple-element.53) | copy-start | bytes 9830404
  178.3 17.1 %collective-permute-start.11 = (bf16[400,256]{1,0:T(8,128)(2,1)S(1)}, bf16[400,256]{1,0:T(8,128)(2,1)S(1)}, u32[]{:S(2)}, u32[]{:S(2)}) collective-permute-start(bf16[400,256]{1,0:T(8,128)(2,1)S(1)} %fusion.34), channel_id=1, source_target_pairs={{0,8},{1,9},{2,10},{3,11},{4,12},{5,13},{6,14},{7,15},{8,0},{9,1},... | collective-permute-start | bytes 614408 | tf_op jit(solution)/shard_map/ppermute | solution.py:117
  184.9 16.1 %collective-permute-start.12 = (bf16[2,2,400,256]{3,2,0,1:T(8,128)(2,1)S(1)}, bf16[2,2,400,256]{3,2,0,1:T(8,128)(2,1)S(1)}, u32[]{:S(2)}, u32[]{:S(2)}) collective-permute-start(bf16[2,2,400,256]{3,2,0,1:T(8,128)(2,1)S(1)} %fusion.20), channel_id=1, source_target_pairs={{0,2},{1,3},{2,0},{3,1},{4,6},{5,7},{6,4},{7,5},{8,10},{9,11},{10,... | collective-permute-start | bytes 2457608 | tf_op jit(solution)/shard_map/ppermute | solution.py:117
  185.9 13.4 %collective-permute-start.10 = (bf16[400,256]{1,0:T(8,128)(2,1)S(1)}, bf16[400,256]{1,0:T(8,128)(2,1)S(1)}, u32[]{:S(2)}, u32[]{:S(2)}) collective-permute-start(bf16[400,256]{1,0:T(8,128)(2,1)S(1)} %fusion.33), channel_id=1, source_target_pairs={{0,8},{1,9},{2,10},{3,11},{4,12},{5,13},{6,14},{7,15},{8,0},{9,1},... | collective-permute-start | bytes 614408 | tf_op jit(solution)/shard_map/ppermute | solution.py:117
  186.1 16.0 %collective-permute-start.13 = (bf16[2,2,400,256]{3,2,0,1:T(8,128)(2,1)S(1)}, bf16[2,2,400,256]{3,2,0,1:T(8,128)(2,1)S(1)}, u32[]{:S(2)}, u32[]{:S(2)}) collective-permute-start(bf16[2,2,400,256]{3,2,0,1:T(8,128)(2,1)S(1)} %fusion.21), channel_id=1, source_target_pairs={{0,1},{1,0},{2,3},{3,2},{4,5},{5,4},{6,7},{7,6},{8,9},{9,8},{10,11... | collective-permute-start | bytes 2457608 | tf_op jit(solution)/shard_map/ppermute | solution.py:117
  202.4 6.0 %collective-permute-start.14 = (bf16[400,128]{1,0:T(8,128)(2,1)S(1)}, bf16[400,128]{1,0:T(8,128)(2,1)S(1)}, u32[]{:S(2)}, u32[]{:S(2)}) collective-permute-start(bf16[400,128]{1,0:T(8,128)(2,1)S(1)} %get-tuple-element.67), channel_id=1, source_target_pairs={{0,8},{1,9},{2,10},{3,11},{4,12},{5,13},{6,14},{7,15},{8,0},{9,1},... | collective-permute-start | bytes 307208 | tf_op jit(solution)/shard_map/ppermute | solution.py:124
  205.1 6.7 %collective-permute-start.15 = (bf16[400,128]{1,0:T(8,128)(2,1)S(1)}, bf16[400,128]{1,0:T(8,128)(2,1)S(1)}, u32[]{:S(2)}, u32[]{:S(2)}) collective-permute-start(bf16[400,128]{1,0:T(8,128)(2,1)S(1)} %get-tuple-element.68), channel_id=1, source_target_pairs={{0,8},{1,9},{2,10},{3,11},{4,12},{5,13},{6,14},{7,15},{8,0},{9,1},... | collective-permute-start | bytes 307208 | tf_op jit(solution)/shard_map/ppermute | solution.py:124
  205.5 13.6 %collective-permute-start.16 = (bf16[2,400,256]{2,1,0:T(8,128)(2,1)S(1)}, bf16[2,400,256]{2,1,0:T(8,128)(2,1)S(1)}, u32[]{:S(2)}, u32[]{:S(2)}) collective-permute-start(bf16[2,400,256]{2,1,0:T(8,128)(2,1)S(1)} %fusion.26), channel_id=1, source_target_pairs={{0,4},{1,5},{2,6},{3,7},{4,0},{5,1},{6,2},{7,3},{8,12},{9,13},{10,... | collective-permute-start | bytes 1228808 | tf_op jit(solution)/shard_map/ppermute | solution.py:117
  207.1 19.2 %collective-permute-start.17 = (bf16[2,400,256]{2,1,0:T(8,128)(2,1)S(1)}, bf16[2,400,256]{2,1,0:T(8,128)(2,1)S(1)}, u32[]{:S(2)}, u32[]{:S(2)}) collective-permute-start(bf16[2,400,256]{2,1,0:T(8,128)(2,1)S(1)} %fusion.27), channel_id=1, source_target_pairs={{0,4},{1,5},{2,6},{3,7},{4,0},{5,1},{6,2},{7,3},{8,12},{9,13},{10,... | collective-permute-start | bytes 1228808 | tf_op jit(solution)/shard_map/ppermute | solution.py:117
  226.4 11.7 %collective-permute-start.18 = (bf16[2,400,128]{2,1,0:T(8,128)(2,1)S(1)}, bf16[2,400,128]{2,1,0:T(8,128)(2,1)S(1)}, u32[]{:S(2)}, u32[]{:S(2)}) collective-permute-start(bf16[2,400,128]{2,1,0:T(8,128)(2,1)S(1)} %pad_maximum_fusion.14), channel_id=1, source_target_pairs={{0,4},{1,5},{2,6},{3,7},{4,0},{5,1},{6,2},{7,3},{8,12},{9,13},{10,... | collective-permute-start | bytes 614408 | tf_op jit(solution)/shard_map/ppermute | solution.py:124
  226.5 23.4 %collective-permute-start.19 = (bf16[2,400,128]{2,1,0:T(8,128)(2,1)S(1)}, bf16[2,400,128]{2,1,0:T(8,128)(2,1)S(1)}, u32[]{:S(2)}, u32[]{:S(2)}) collective-permute-start(bf16[2,400,128]{2,1,0:T(8,128)(2,1)S(1)} %pad_maximum_fusion.15), channel_id=1, source_target_pairs={{0,4},{1,5},{2,6},{3,7},{4,0},{5,1},{6,2},{7,3},{8,12},{9,13},{10,... | collective-permute-start | bytes 614408 | tf_op jit(solution)/shard_map/ppermute | solution.py:124
  228.5 18.3 %collective-permute-start.21 = (bf16[400,256]{1,0:T(8,128)(2,1)S(1)}, bf16[400,256]{1,0:T(8,128)(2,1)S(1)}, u32[]{:S(2)}, u32[]{:S(2)}) collective-permute-start(bf16[400,256]{1,0:T(8,128)(2,1)S(1)} %fusion.36), channel_id=1, source_target_pairs={{0,8},{1,9},{2,10},{3,11},{4,12},{5,13},{6,14},{7,15},{8,0},{9,1},... | collective-permute-start | bytes 614408 | tf_op jit(solution)/shard_map/ppermute | solution.py:117
  228.7 21.0 %collective-permute-start.20 = (bf16[400,256]{1,0:T(8,128)(2,1)S(1)}, bf16[400,256]{1,0:T(8,128)(2,1)S(1)}, u32[]{:S(2)}, u32[]{:S(2)}) collective-permute-start(bf16[400,256]{1,0:T(8,128)(2,1)S(1)} %fusion.35), channel_id=1, source_target_pairs={{0,8},{1,9},{2,10},{3,11},{4,12},{5,13},{6,14},{7,15},{8,0},{9,1},... | collective-permute-start | bytes 614408 | tf_op jit(solution)/shard_map/ppermute | solution.py:117
  250.0 6.7 %collective-permute-start.24 = (bf16[400,128]{1,0:T(8,128)(2,1)S(1)}, bf16[400,128]{1,0:T(8,128)(2,1)S(1)}, u32[]{:S(2)}, u32[]{:S(2)}) collective-permute-start(bf16[400,128]{1,0:T(8,128)(2,1)S(1)} %get-tuple-element.77), channel_id=1, source_target_pairs={{0,8},{1,9},{2,10},{3,11},{4,12},{5,13},{6,14},{7,15},{8,0},{9,1},... | collective-permute-start | bytes 307208 | tf_op jit(solution)/shard_map/ppermute | solution.py:124
  250.1 10.0 %collective-permute-start.22 = (bf16[2,2,400,128]{3,2,0,1:T(8,128)(2,1)S(1)}, bf16[2,2,400,128]{3,2,0,1:T(8,128)(2,1)S(1)}, u32[]{:S(2)}, u32[]{:S(2)}) collective-permute-start(bf16[2,2,400,128]{3,2,0,1:T(8,128)(2,1)S(1)} %pad_maximum_fusion.10), channel_id=1, source_target_pairs={{0,2},{1,3},{2,0},{3,1},{4,6},{5,7},{6,4},{7,5},{8,10},{9,11},{10,... | collective-permute-start | bytes 1228808 | tf_op jit(solution)/shard_map/ppermute | solution.py:124
  250.6 9.7 %collective-permute-start.23 = (bf16[2,2,400,128]{3,2,1,0:T(8,128)(2,1)S(1)}, bf16[2,2,400,128]{3,2,1,0:T(8,128)(2,1)S(1)}, u32[]{:S(2)}, u32[]{:S(2)}) collective-permute-start(bf16[2,2,400,128]{3,2,1,0:T(8,128)(2,1)S(1)} %pad_maximum_fusion.11), channel_id=1, source_target_pairs={{0,1},{1,0},{2,3},{3,2},{4,5},{5,4},{6,7},{7,6},{8,9},{9,8},{10,11... | collective-permute-start | bytes 1228808 | tf_op jit(solution)/shard_map/ppermute | solution.py:124
  251.5 6.3 %collective-permute-start.25 = (bf16[400,128]{1,0:T(8,128)(2,1)S(1)}, bf16[400,128]{1,0:T(8,128)(2,1)S(1)}, u32[]{:S(2)}, u32[]{:S(2)}) collective-permute-start(bf16[400,128]{1,0:T(8,128)(2,1)S(1)} %get-tuple-element.78), channel_id=1, source_target_pairs={{0,8},{1,9},{2,10},{3,11},{4,12},{5,13},{6,14},{7,15},{8,0},{9,1},... | collective-permute-start | bytes 307208 | tf_op jit(solution)/shard_map/ppermute | solution.py:124
  260.5 6.4 %collective-permute-start.28 = (bf16[2,400,128]{2,1,0:T(8,128)(2,1)S(1)}, bf16[2,400,128]{2,1,0:T(8,128)(2,1)S(1)}, u32[]{:S(2)}, u32[]{:S(2)}) collective-permute-start(bf16[2,400,128]{2,1,0:T(8,128)(2,1)S(1)} %pad_maximum_fusion.16), channel_id=1, source_target_pairs={{0,4},{1,5},{2,6},{3,7},{4,0},{5,1},{6,2},{7,3},{8,12},{9,13},{10,... | collective-permute-start | bytes 614408 | tf_op jit(solution)/shard_map/ppermute | solution.py:124
  260.5 17.8 %collective-permute-start.26 = (bf16[2,2,2,400,128]{4,3,0,1,2:T(8,128)(2,1)S(1)}, bf16[2,2,2,400,128]{4,3,0,1,2:T(8,128)(2,1)S(1)}, u32[]{:S(2)}, u32[]{:S(2)}) collective-permute-start(bf16[2,2,2,400,128]{4,3,0,1,2:T(8,128)(2,1)S(1)} %pad_maximum_fusion.4), channel_id=1, source_target_pairs={{0,1},{1,0},{2,3},{3,2},{4,5},{5,4},{6,7},{7,6},{8,9},{9,8},{10,11... | collective-permute-start | bytes 2457608 | tf_op jit(solution)/shard_map/ppermute | solution.py:124
  261.2 61.9 %collective-permute-start.34 = (bf16[16,224,512]{2,1,0:T(8,128)(2,1)}, bf16[16,224,512]{2,1,0:T(8,128)(2,1)}, u32[]{:S(2)}, u32[]{:S(2)}) collective-permute-start(bf16[16,224,512]{2,1,0:T(8,128)(2,1)} %get-tuple-element.95), channel_id=1, source_target_pairs={{0,16},{16,0},{1,17},{17,1},{2,18},{18,2},{3,19},{19,3},{4,20},{20... | collective-permute-start | bytes 11010056 | tf_op jit(solution)/shard_map/ppermute | solution.py:175
  261.2 20.7 %collective-permute-start.27 = (bf16[2,2,2,400,128]{4,3,2,1,0:T(8,128)(2,1)S(1)}, bf16[2,2,2,400,128]{4,3,2,1,0:T(8,128)(2,1)S(1)}, u32[]{:S(2)}, u32[]{:S(2)}) collective-permute-start(bf16[2,2,2,400,128]{4,3,2,1,0:T(8,128)(2,1)S(1)} %pad_maximum_fusion.5), channel_id=1, source_target_pairs={{0,2},{1,3},{2,0},{3,1},{4,6},{5,7},{6,4},{7,5},{8,10},{9,11},{10,... | collective-permute-start | bytes 2457608 | tf_op jit(solution)/shard_map/ppermute | solution.py:124
  262.6 8.1 %collective-permute-start.29 = (bf16[2,400,128]{2,1,0:T(8,128)(2,1)S(1)}, bf16[2,400,128]{2,1,0:T(8,128)(2,1)S(1)}, u32[]{:S(2)}, u32[]{:S(2)}) collective-permute-start(bf16[2,400,128]{2,1,0:T(8,128)(2,1)S(1)} %pad_maximum_fusion.17), channel_id=1, source_target_pairs={{0,4},{1,5},{2,6},{3,7},{4,0},{5,1},{6,2},{7,3},{8,12},{9,13},{10,... | collective-permute-start | bytes 614408 | tf_op jit(solution)/shard_map/ppermute | solution.py:124
  282.1 11.2 %collective-permute-start.30 = (bf16[2,2,400,128]{3,2,0,1:T(8,128)(2,1)S(1)}, bf16[2,2,400,128]{3,2,0,1:T(8,128)(2,1)S(1)}, u32[]{:S(2)}, u32[]{:S(2)}) collective-permute-start(bf16[2,2,400,128]{3,2,0,1:T(8,128)(2,1)S(1)} %pad_maximum_fusion.12), channel_id=1, source_target_pairs={{0,2},{1,3},{2,0},{3,1},{4,6},{5,7},{6,4},{7,5},{8,10},{9,11},{10,... | collective-permute-start | bytes 1228808 | tf_op jit(solution)/shard_map/ppermute | solution.py:124
  283.6 10.8 %collective-permute-start.31 = (bf16[2,2,400,128]{3,2,1,0:T(8,128)(2,1)S(1)}, bf16[2,2,400,128]{3,2,1,0:T(8,128)(2,1)S(1)}, u32[]{:S(2)}, u32[]{:S(2)}) collective-permute-start(bf16[2,2,400,128]{3,2,1,0:T(8,128)(2,1)S(1)} %pad_maximum_fusion.13), channel_id=1, source_target_pairs={{0,1},{1,0},{2,3},{3,2},{4,5},{5,4},{6,7},{7,6},{8,9},{9,8},{10,11... | collective-permute-start | bytes 1228808 | tf_op jit(solution)/shard_map/ppermute | solution.py:124
  295.4 19.2 %collective-permute-start.32 = (bf16[2,2,2,400,128]{4,3,0,1,2:T(8,128)(2,1)}, bf16[2,2,2,400,128]{4,3,0,1,2:T(8,128)(2,1)}, u32[]{:S(2)}, u32[]{:S(2)}) collective-permute-start(bf16[2,2,2,400,128]{4,3,0,1,2:T(8,128)(2,1)} %pad_maximum_fusion.6), channel_id=1, source_target_pairs={{0,1},{1,0},{2,3},{3,2},{4,5},{5,4},{6,7},{7,6},{8,9},{9,8},{10,11... | collective-permute-start | bytes 2457608 | tf_op jit(solution)/shard_map/ppermute | solution.py:124
  297.0 19.3 %collective-permute-start.33 = (bf16[2,2,2,400,128]{4,3,2,1,0:T(8,128)(2,1)}, bf16[2,2,2,400,128]{4,3,2,1,0:T(8,128)(2,1)}, u32[]{:S(2)}, u32[]{:S(2)}) collective-permute-start(bf16[2,2,2,400,128]{4,3,2,1,0:T(8,128)(2,1)} %pad_maximum_fusion.7), channel_id=1, source_target_pairs={{0,2},{1,3},{2,0},{3,1},{4,6},{5,7},{6,4},{7,5},{8,10},{9,11},{10,... | collective-permute-start | bytes 2457608 | tf_op jit(solution)/shard_map/ppermute | solution.py:124
  358.6 4.0 %copy-start.9 = (f32[2,768,224]{2,1,0:T(8,128)S(1)}, f32[2,768,224]{2,1,0:T(8,128)}, u32[]{:S(2)}) copy-start(f32[2,768,224]{2,1,0:T(8,128)} %shard_map.66) | copy-start | bytes 4128772
  358.9 2.3 collective-permute-start.35
